TPU v7x, 256 devices: a whole 4x4x8 slice. The times are simulated.
256 devices in a mesh: slab: 4 (over x), row: 8 (over y, z_hi), col: 8 (over z_lo, core).
Axes of the slice: x: 4, y: 4, z: 8 (z_hi: 2, z_lo: 4; z = z_hi * 4 + z_lo), core: 2. Of those that a mesh axis runs over, the one named last changes fastest.
Arguments:
- wave: float32 [16, 32, 64, 1024], P(None, 'slab', 'row', 'col')
- potential: float32 [32, 64, 1024], P('slab', 'row', 'col'), may hold values from -1 to 1
- positions: int32 [3, 2048], P(None, ('slab', 'row', 'col')), may hold values from 0 to 1023, as said below
- species: int32 [2048], P(('slab', 'row', 'col')), may hold values from 0 to 3
- counts: int32 [256], P(('slab', 'row', 'col')), may hold values from 1 to 8, as said below
- offsets: int32 [4, 3, 384], replicated, may hold values from -5 to 5, as said below
- beta: float32 [4, 384], replicated, may hold values from -0.3125 to 0.3125
- coupling: float32 [4], replicated, may hold values from 0.5 to 4
Outputs:
- filtered: float32 [16, 32, 64, 1024], P(None, 'slab', 'row', 'col')
- gram: float32 [16, 16], replicated
Inputs may be any that keep to these rules, and one draw needn't show every extreme that they name: `positions`: slot j belongs to block j // 8, blocks numbered with the first dimension slowest and the third fastest; its position lies inside that block of 8 x 8 x 128 cells; the first slot sits at the grid's first cell and the last slot at its last cell. `counts`: some block has all 8 slots live. `offsets`: each species' points are distinct lattice points at distance 5 or less from the anchor, and include the six points at distance 5 along the axes.
All inputs are finite; a program needn't handle non-finite values.
Results may differ from a plain program's by a relative error of at most 0.000086.
Values sent between devices are 32-bit elements; how exact they have to be, the bound alone decides.
No kernel may reach another device: no remote copies, remote signals or barrier semaphores. Data moves between devices by JAX's collectives and lax.ppermute only.
A program may use at most 192 MiB of HBM per device.

v0:
```python
import jax
import jax.numpy as jnp
from jax import lax
from jax.sharding import PartitionSpec as P

stencil_weights = (
    -5369.0 / 1800.0,
    12.0 / 7.0,
    -15.0 / 56.0,
    10.0 / 189.0,
    -1.0 / 112.0,
    2.0 / 1925.0,
    -1.0 / 16632.0,
)
lower_edge = 3.0
upper_edge = 17.0


def padded_2(block, sides, width):
    for axis, dim in sides:
        count = lax.axis_size(axis)
        forward = [(i, i + 1) for i in range(count - 1)]
        backward = [(target, source) for source, target in forward]
        low = lax.ppermute(
            lax.slice_in_dim(block, block.shape[dim] - width, None, axis=dim), axis, forward
        )
        high = lax.ppermute(lax.slice_in_dim(block, 0, width, axis=dim), axis, backward)
        block = jnp.concatenate([low, block, high], axis=dim)
    return block


def stencil(padded, extent):
    size_x, size_y, size_z = extent

    def window(shift_x, shift_y, shift_z):
        return padded[
            :,
            6 + shift_x : 6 + shift_x + size_x,
            6 + shift_y : 6 + shift_y + size_y,
            6 + shift_z : 6 + shift_z + size_z,
        ]

    total = 3.0 * stencil_weights[0] * window(0, 0, 0)
    for reach in range(1, 7):
        paired = (
            window(reach, 0, 0)
            + window(-reach, 0, 0)
            + window(0, reach, 0)
            + window(0, -reach, 0)
            + window(0, 0, reach)
            + window(0, 0, -reach)
        )
        total = total + stencil_weights[reach] * paired
    return total


def atom_tables(species, offsets, beta, coupling):
    matches = species[:, None] == jnp.arange(beta.shape[0], dtype=jnp.int32)[None]
    onehot = matches.astype(jnp.float32)
    shapes = jnp.dot(onehot, beta, precision=lax.Precision.HIGHEST)
    gains = jnp.sum(onehot * coupling[None], axis=1)
    offset_rows = jnp.sum(jnp.where(matches[:, :, None, None], offsets[None], 0), axis=1)
    return (shapes, offset_rows, gains)


def add_rims(accumulated, received, axis_dim):
    length = accumulated.shape[axis_dim]
    inner = lax.slice_in_dim(accumulated, 6, length - 6, axis=axis_dim)
    lower_part = lax.slice_in_dim(received, 0, 6, axis=axis_dim)
    upper_part = lax.slice_in_dim(received, 18, 24, axis=axis_dim)
    leading = [slice(None)] * 4
    leading[axis_dim] = slice(0, 6)
    inner = inner.at[tuple(leading)].add(lower_part)
    trailing = [slice(None)] * 4
    trailing[axis_dim] = slice(length - 18, length - 12)
    return inner.at[tuple(trailing)].add(upper_part)


def shards(wave, potential, positions, species, counts, offsets, beta, coupling):
    bands, size_x, size_y, size_z = wave.shape
    extent = (size_x, size_y, size_z)
    wide_x, wide_y, wide_z = (size_x + 12, size_y + 12, size_z + 12)
    anchor = jnp.stack(
        [
            lax.axis_index("slab") * size_x,
            lax.axis_index("row") * size_y,
            lax.axis_index("col") * size_z,
        ]
    )
    slot_count = positions.shape[1]
    own_shapes, own_offsets, own_gains = atom_tables(species, offsets, beta, coupling)
    active = (jnp.arange(slot_count, dtype=jnp.int32) < counts[0]).astype(jnp.float32)
    own_weights = own_gains * active
    local = positions.T[:, :, None] - anchor[None, :, None] + own_offsets + 6
    ext_index = ((local[:, 0] * wide_y + local[:, 1]) * wide_z + local[:, 2]).reshape(-1)
    centre = 0.5 * (upper_edge + lower_edge)
    half_width = 0.5 * (upper_edge - lower_edge)

    def spread_rims(scaled):
        contributions = (scaled[:, :, None] * own_shapes[None]).reshape(bands, -1)
        accumulated = (
            jnp.zeros((bands, wide_x * wide_y * wide_z), jnp.float32)
            .at[:, ext_index]
            .add(contributions)
        )
        accumulated = accumulated.reshape(bands, wide_x, wide_y, wide_z)
        rims = jnp.concatenate([accumulated[:, :6], accumulated[:, -6:]], axis=1)
        received = padded_2(rims, (("slab", 1),), 6)
        accumulated = add_rims(accumulated, received, 1)
        rims = jnp.concatenate([accumulated[:, :, :6], accumulated[:, :, -6:]], axis=2)
        received = padded_2(rims, (("row", 2),), 6)
        accumulated = add_rims(accumulated, received, 2)
        rims = jnp.concatenate([accumulated[:, :, :, :6], accumulated[:, :, :, -6:]], axis=3)
        received = padded_2(rims, (("col", 3),), 6)
        return add_rims(accumulated, received, 3)

    def filter_step(field):
        padded = padded_2(field, (("slab", 1), ("row", 2), ("col", 3)), 6)
        picked = jnp.take(padded.reshape(bands, -1), ext_index, axis=1).reshape(
            bands, slot_count, -1
        )
        projected = jnp.sum(picked * own_shapes[None], axis=2)
        scaled = projected * own_weights[None]
        projector_part = spread_rims(scaled)
        applied = -0.5 * stencil(padded, extent) + potential[None] * field + projector_part
        return (applied - centre * field) / half_width

    first = filter_step(wave)
    second = 2.0 * filter_step(first) - wave
    third = 2.0 * filter_step(second) - first
    flattened = third.reshape(bands, -1)
    partial_gram = jnp.dot(flattened, flattened.T, precision=lax.Precision.HIGHEST)
    summed_gram = lax.psum(partial_gram, ("slab", "row", "col"))
    cells_total = (
        size_x
        * size_y
        * size_z
        * lax.axis_size("slab")
        * lax.axis_size("row")
        * lax.axis_size("col")
    )
    return (third, summed_gram / cells_total)


def solution(mesh):
    in_specs = (
        P(None, "slab", "row", "col"),
        P("slab", "row", "col"),
        P(None, ("slab", "row", "col")),
        P(("slab", "row", "col")),
        P(("slab", "row", "col")),
        P(),
        P(),
        P(),
    )
    out_specs = (P(None, "slab", "row", "col"), P())
    return jax.shard_map(shards, mesh=mesh, in_specs=in_specs, out_specs=out_specs, check_vma=False)
```

profile of v0, /device:TPU:1, one launch (start us, length us, event | category | flops | bytes accessed | tf_op | source)
XLA Modules:
  0.0 1409.3 jit_solution(11997852281129113231)
XLA Ops:
  21.2 9.5 collective-permute-start.3
  30.9 20.1 %collective-permute-done.2 = f32[16,20,6,128]{3,0,2,1:T(8,128)S(1)} collective-permute-done((f32[16,20,6,128]{3,0,2,1:T(8,128)S(1)}, f32[16,20,6,128]{3,0,2,1:T(8,128)S(1)}, u32[]{:S(2)}, u32[]{:S(2)}) %collective-permute-start.2) | collective-permute-done | bytes 983072 | tf_op jit(solution)/shard_map/ppermute | solution.py:27
  65.0 5.3 collective-permute-start.4
  75.0 25.6 %collective-permute-start.5 = (f32[16,20,20,6]{2,0,3,1:T(8,128)}, f32[16,20,20,6]{2,0,3,1:T(8,128)}, u32[]{:S(2)}, u32[]{:S(2)}) collective-permute-start(f32[16,20,20,6]{2,0,3,1:T(8,128)} %copy.117), channel_id=1, source_target_pairs={{0,1},{1,2},{2,3},{3,4},{4,5},{5,6},{6,7},{8,9},{9,10},{10,11},{11... | collective-permute-start | bytes 460808 | tf_op jit(solution)/shard_map/ppermute | solution.py:24
  100.6 5.3 collective-permute-done.4
  110.3 12.4 collective-permute-done.5
  127.1 10.1 pad_maximum_fusion
  137.3 6.3 reshape.786
  143.5 14.7 %copy.122 = f32[16,56000]{0,1:T(8,128)} copy(f32[16,56000]{1,0:T(8,128)} %reshape.786) | data formatting | bytes 7168000 | tf_op jit(solution)/shard_map/reshape | solution.py:119
  158.3 20.0 %gather_fusion = f32[3072,16]{1,0:T(8,128)} fusion(f32[16,56000]{0,1:T(8,128)} %copy.122, s32[3072]{0:T(1024)S(1)} %fusion.179), kind=kCustom, calls=%fused_computation.clone | custom fusion | bytes 405504 | tf_op jit(solution)/shard_map/jit(_take)/gather | solution.py:119
  183.1 27.5 %scatter_custom_fusion = f32[16,56000]{0,1:T(8,128)} fusion(s32[3072]{0:T(1024)S(1)} %bitcast.54, f32[]{:T(128)} %constant.455.clone.1, f32[16,3072]{0,1:T(8,128)} %bitcast_multiply_fusion.2), kind=kCustom, calls=%fused_computation.10 | custom fusion | flops 49152 | bytes 3780612 | tf_op jit(solution)/shard_map/scatter-add | solution.py:104
  210.6 16.5 %copy.123 = f32[16,56000]{1,0:T(8,128)} copy(f32[16,56000]{0,1:T(8,128)} %scatter_custom_fusion) | data formatting | bytes 7168000 | tf_op jit(solution)/shard_map/scatter-add | solution.py:104
  227.1 8.4 reshape.788
  245.5 18.7 %collective-permute-done.6 = f32[16,6,20,140]{3,0,2,1:T(8,128)S(1)} collective-permute-done((f32[16,6,20,140]{3,0,2,1:T(8,128)S(1)}, f32[16,6,20,140]{3,0,2,1:T(8,128)S(1)}, u32[]{:S(2)}, u32[]{:S(2)}) %collective-permute-start.6) | collective-permute-done | bytes 1075232 | tf_op jit(solution)/shard_map/ppermute | solution.py:24
  271.9 24.8 %collective-permute-start.8 = (f32[16,8,6,140]{3,1,2,0:T(8,128)S(1)}, f32[16,8,6,140]{3,1,2,0:T(8,128)S(1)}, u32[]{:S(2)}, u32[]{:S(2)}) collective-permute-start(f32[16,8,6,140]{3,1,2,0:T(8,128)S(1)} %copy.128), channel_id=1, source_target_pairs={{0,8},{8,16},{16,24},{24,32},{32,40},{40,48},{48,56},{1,9},{9,17},... | collective-permute-start | bytes 1290248 | tf_op jit(solution)/shard_map/ppermute | solution.py:24
  299.4 6.0 collective-permute-done.8
  306.9 6.4 scatter-add.85
  313.3 51.1 %collective-permute-done.9 = f32[16,8,6,140]{3,1,2,0:T(8,128)} collective-permute-done((f32[16,8,6,140]{3,1,2,0:T(8,128)S(1)}, f32[16,8,6,140]{3,1,2,0:T(8,128)}, u32[]{:S(2)}, u32[]{:S(2)}) %collective-permute-start.9) | collective-permute-done | bytes 430112 | tf_op jit(solution)/shard_map/ppermute | solution.py:27
  367.2 6.4 scatter-add.86
  375.9 11.2 collective-permute-start.10
  401.4 21.4 %scatter-add.90 = f32[16,8,8,128]{3,2,1,0:T(8,128)S(1)} dynamic-update-slice(f32[16,8,8,128]{3,2,1,0:T(8,128)S(1)} %scatter-add.89, f32[16,8,8,6]{3,2,1,0:T(8,128)} %slice_add_fusion.20, s32[]{:T(128)} %constant.461.clone.1, s32[]{:T(128)} %constant.461.clone.1, s32[]{:T(128)} %constant.461.clone.1, s32[]{:T(128)} %constant.467.clone.1) | dynamic-update-slice | bytes 49156 | tf_op jit(solution)/shard_map/scatter-add | solution.py:76
  423.6 15.8 %broadcast_multiply_fusion = (f32[16,8,8,128]{3,2,1,0:T(8,128)S(1)}, f32[16,8,8,128]{3,2,1,0:T(8,128)}) fusion(f32[16,8,8,128]{3,2,1,0:T(8,128)} %param.46, f32[16,8,8,128]{3,2,1,0:T(8,128)} %copy-done.12, f32[8,8,128]{2,1,0:T(8,128)S(1)} %copy-done.17, f32[16,20,6,128]{3,2,1,0:T(8,128)S(1)} %copy.110, f32[16,20,8,128]{3,2,1,0:T(8,128)S(1)} %get-tuple-element.265, ...), kind=kLoop, calls=%fused_computation.326 | loop fusion | flops 12845056 | bytes 12005376 | tf_op jit(solution)/shard_map/div | solution.py:126
  452.3 18.1 %collective-permute-start.15 = (f32[16,20,6,128]{3,0,2,1:T(8,128)S(1)}, f32[16,20,6,128]{3,0,2,1:T(8,128)S(1)}, u32[]{:S(2)}, u32[]{:S(2)}) collective-permute-start(f32[16,20,6,128]{3,0,2,1:T(8,128)S(1)} %copy.134), channel_id=1, source_target_pairs={{0,8},{8,16},{16,24},{24,32},{32,40},{40,48},{48,56},{1,9},{9,17},... | collective-permute-start | bytes 2949128 | tf_op jit(solution)/shard_map/ppermute | solution.py:24
  470.4 19.6 %collective-permute-done.14 = f32[16,20,6,128]{3,0,2,1:T(8,128)S(1)} collective-permute-done((f32[16,20,6,128]{3,0,2,1:T(8,128)S(1)}, f32[16,20,6,128]{3,0,2,1:T(8,128)S(1)}, u32[]{:S(2)}, u32[]{:S(2)}) %collective-permute-start.14) | collective-permute-done | bytes 983072 | tf_op jit(solution)/shard_map/ppermute | solution.py:27
  507.1 24.5 %collective-permute-start.17 = (f32[16,20,20,6]{2,0,3,1:T(8,128)}, f32[16,20,20,6]{2,0,3,1:T(8,128)}, u32[]{:S(2)}, u32[]{:S(2)}) collective-permute-start(f32[16,20,20,6]{2,0,3,1:T(8,128)} %copy.140), channel_id=1, source_target_pairs={{0,1},{1,2},{2,3},{3,4},{4,5},{5,6},{6,7},{8,9},{9,10},{10,11},{11... | collective-permute-start | bytes 460808 | tf_op jit(solution)/shard_map/ppermute | solution.py:24
  531.6 5.1 collective-permute-done.16
  541.1 19.1 %collective-permute-done.17 = f32[16,20,20,6]{2,0,3,1:T(8,128)} collective-permute-done((f32[16,20,20,6]{2,0,3,1:T(8,128)}, f32[16,20,20,6]{2,0,3,1:T(8,128)}, u32[]{:S(2)}, u32[]{:S(2)}) %collective-permute-start.17) | collective-permute-done | bytes 153632 | tf_op jit(solution)/shard_map/ppermute | solution.py:24
  564.7 10.9 pad_maximum_fusion.1
  575.6 6.3 reshape.789
  581.9 14.7 %copy.144 = f32[16,56000]{0,1:T(8,128)} copy(f32[16,56000]{1,0:T(8,128)} %reshape.789) | data formatting | bytes 7168000 | tf_op jit(solution)/shard_map/reshape | solution.py:119
  596.6 21.0 %gather_fusion.1 = f32[3072,16]{1,0:T(8,128)} fusion(f32[16,56000]{0,1:T(8,128)} %copy.144, s32[3072]{0:T(1024)} %copy-done.22), kind=kCustom, calls=%fused_computation.1.clone | custom fusion | bytes 405504 | tf_op jit(solution)/shard_map/jit(_take)/gather | solution.py:119
  622.5 27.2 %scatter_custom_fusion.1 = f32[16,56000]{0,1:T(8,128)} fusion(s32[3072]{0:T(1024)} %bitcast.55, f32[]{:T(128)} %constant.455.clone.1, f32[16,3072]{0,1:T(8,128)} %bitcast_multiply_fusion.1), kind=kCustom, calls=%fused_computation.8 | custom fusion | flops 49152 | bytes 5157376 | tf_op jit(solution)/shard_map/scatter-add | solution.py:104
  649.7 16.5 %copy.145 = f32[16,56000]{1,0:T(8,128)} copy(f32[16,56000]{0,1:T(8,128)} %scatter_custom_fusion.1) | data formatting | bytes 7168000 | tf_op jit(solution)/shard_map/scatter-add | solution.py:104
  666.1 8.4 reshape.791
  685.6 18.7 %collective-permute-done.18 = f32[16,6,20,140]{3,0,2,1:T(8,128)S(1)} collective-permute-done((f32[16,6,20,140]{3,0,2,1:T(8,128)S(1)}, f32[16,6,20,140]{3,0,2,1:T(8,128)S(1)}, u32[]{:S(2)}, u32[]{:S(2)}) %collective-permute-start.18) | collective-permute-done | bytes 1075232 | tf_op jit(solution)/shard_map/ppermute | solution.py:24
  712.0 17.7 %collective-permute-start.20 = (f32[16,8,6,140]{3,1,2,0:T(8,128)S(1)}, f32[16,8,6,140]{3,1,2,0:T(8,128)S(1)}, u32[]{:S(2)}, u32[]{:S(2)}) collective-permute-start(f32[16,8,6,140]{3,1,2,0:T(8,128)S(1)} %copy.150), channel_id=1, source_target_pairs={{0,8},{8,16},{16,24},{24,32},{32,40},{40,48},{48,56},{1,9},{9,17},... | collective-permute-start | bytes 1290248 | tf_op jit(solution)/shard_map/ppermute | solution.py:24
  739.7 6.4 scatter-add.96
  746.1 57.5 %collective-permute-done.21 = f32[16,8,6,140]{3,1,2,0:T(8,128)} collective-permute-done((f32[16,8,6,140]{3,1,2,0:T(8,128)}, f32[16,8,6,140]{3,1,2,0:T(8,128)}, u32[]{:S(2)}, u32[]{:S(2)}) %collective-permute-start.21) | collective-permute-done | bytes 430112 | tf_op jit(solution)/shard_map/ppermute | solution.py:27
  806.5 6.4 scatter-add.99
  815.0 16.4 %collective-permute-start.22 = (f32[16,8,8,6]{3,2,1,0:T(8,128)S(1)}, f32[16,8,8,6]{3,2,1,0:T(8,128)S(1)}, u32[]{:S(2)}, u32[]{:S(2)}) collective-permute-start(f32[16,8,8,6]{3,2,1,0:T(8,128)S(1)} %get-tuple-element.252), channel_id=1, source_target_pairs={{0,1},{1,2},{2,3},{3,4},{4,5},{5,6},{6,7},{8,9},{9,10},{10,11},{11... | collective-permute-start | bytes 73736 | tf_op jit(solution)/shard_map/ppermute | solution.py:24
  848.7 21.4 %scatter-add.101 = f32[16,8,8,128]{3,2,1,0:T(8,128)S(1)} dynamic-update-slice(f32[16,8,8,128]{3,2,1,0:T(8,128)S(1)} %scatter-add.100, f32[16,8,8,6]{3,2,1,0:T(8,128)} %slice_add_fusion.16, s32[]{:T(128)} %constant.461.clone.1, s32[]{:T(128)} %constant.461.clone.1, s32[]{:T(128)} %constant.461.clone.1, s32[]{:T(128)} %constant.467.clone.1) | dynamic-update-slice | bytes 49156 | tf_op jit(solution)/shard_map/scatter-add | solution.py:76
  870.8 17.1 %fusion.81 = f32[16,8,8,128]{3,2,1,0:T(8,128)S(1)} fusion(f32[16,8,8,128]{3,2,1,0:T(8,128)} %param.46, f32[16,8,8,128]{3,2,1,0:T(8,128)} %copy-done.13, f32[16,8,8,128]{3,2,1,0:T(8,128)} %copy-done.2, f32[16,6,8,128]{3,2,1,0:T(8,128)} %copy-done.11, f32[16,6,8,128]{3,2,1,0:T(8,128)S(1)} %collective-permute-done.12, f32[16,20,20,6]{3,2,1,0:T(8,128)} %copy.141, ...), kind=kLoop, calls=%fused_computation.181 | loop fusion | flops 16121856 | bytes 12005376 | tf_op jit(solution)/shard_map/sub | solution.py:129
  900.9 8.0 collective-permute-start.27
  908.9 19.6 %collective-permute-done.26 = f32[16,20,6,128]{3,0,2,1:T(8,128)S(1)} collective-permute-done((f32[16,20,6,128]{3,0,2,1:T(8,128)S(1)}, f32[16,20,6,128]{3,0,2,1:T(8,128)S(1)}, u32[]{:S(2)}, u32[]{:S(2)}) %collective-permute-start.26) | collective-permute-done | bytes 983072 | tf_op jit(solution)/shard_map/ppermute | solution.py:27
  934.3 4.7 copy.160
  945.6 5.8 collective-permute-start.29
  951.4 7.0 collective-permute-done.28
  967.3 10.9 pad_maximum_fusion.2
  978.2 6.3 reshape.792
  984.5 14.7 %copy.166 = f32[16,56000]{0,1:T(8,128)} copy(f32[16,56000]{1,0:T(8,128)} %reshape.792) | data formatting | bytes 7168000 | tf_op jit(solution)/shard_map/reshape | solution.py:119
  999.2 21.0 %gather_fusion.2 = f32[3072,16]{1,0:T(8,128)} fusion(f32[16,56000]{0,1:T(8,128)} %copy.166, s32[3072]{0:T(1024)} %copy-done.22), kind=kCustom, calls=%fused_computation.2.clone | custom fusion | bytes 405504 | tf_op jit(solution)/shard_map/jit(_take)/gather | solution.py:119
  1025.1 27.2 %scatter_custom_fusion.2 = f32[16,56000]{0,1:T(8,128)} fusion(s32[3072]{0:T(1024)} %bitcast.56, f32[]{:T(128)} %constant.455.clone.1, f32[16,3072]{0,1:T(8,128)} %bitcast_multiply_fusion), kind=kCustom, calls=%fused_computation.6 | custom fusion | flops 49152 | bytes 5157376 | tf_op jit(solution)/shard_map/scatter-add | solution.py:104
  1052.3 16.5 %copy.167 = f32[16,56000]{1,0:T(8,128)} copy(f32[16,56000]{0,1:T(8,128)} %scatter_custom_fusion.2) | data formatting | bytes 7168000 | tf_op jit(solution)/shard_map/scatter-add | solution.py:104
  1068.8 8.4 reshape.794
  1088.3 30.6 %collective-permute-done.30 = f32[16,6,20,140]{3,0,2,1:T(8,128)S(1)} collective-permute-done((f32[16,6,20,140]{3,0,2,1:T(8,128)S(1)}, f32[16,6,20,140]{3,0,2,1:T(8,128)S(1)}, u32[]{:S(2)}, u32[]{:S(2)}) %collective-permute-start.30) | collective-permute-done | bytes 1075232 | tf_op jit(solution)/shard_map/ppermute | solution.py:24
  1126.9 38.6 %collective-permute-start.32 = (f32[16,8,6,140]{3,1,2,0:T(8,128)S(1)}, f32[16,8,6,140]{3,1,2,0:T(8,128)S(1)}, u32[]{:S(2)}, u32[]{:S(2)}) collective-permute-start(f32[16,8,6,140]{3,1,2,0:T(8,128)S(1)} %copy.172), channel_id=1, source_target_pairs={{0,8},{8,16},{16,24},{24,32},{32,40},{40,48},{48,56},{1,9},{9,17},... | collective-permute-start | bytes 1290248 | tf_op jit(solution)/shard_map/ppermute | solution.py:24
  1169.1 7.1 collective-permute-done.32
  1177.7 6.4 scatter-add.128
  1184.1 33.0 %collective-permute-done.33 = f32[16,8,6,140]{3,1,2,0:T(8,128)} collective-permute-done((f32[16,8,6,140]{3,1,2,0:T(8,128)}, f32[16,8,6,140]{3,1,2,0:T(8,128)}, u32[]{:S(2)}, u32[]{:S(2)}) %collective-permute-start.33) | collective-permute-done | bytes 430112 | tf_op jit(solution)/shard_map/ppermute | solution.py:27
  1220.0 6.4 scatter-add.129
  1245.4 17.9 %collective-permute-done.35 = f32[16,8,8,6]{3,2,1,0:T(8,128)} collective-permute-done((f32[16,8,8,6]{3,2,1,0:T(8,128)}, f32[16,8,8,6]{3,2,1,0:T(8,128)}, u32[]{:S(2)}, u32[]{:S(2)}) %collective-permute-start.35) | collective-permute-done | bytes 24608 | tf_op jit(solution)/shard_map/ppermute | solution.py:27
  1265.5 21.3 %scatter-add.131 = f32[16,8,8,128]{3,2,1,0:T(8,128)} dynamic-update-slice(f32[16,8,8,128]{3,2,1,0:T(8,128)} %scatter-add.130, f32[16,8,8,6]{3,2,1,0:T(8,128)} %slice_add_fusion.12, s32[]{:T(128)} %constant.461.clone.1, s32[]{:T(128)} %constant.461.clone.1, s32[]{:T(128)} %constant.461.clone.1, s32[]{:T(128)} %constant.467.clone.1) | dynamic-update-slice | bytes 49156 | tf_op jit(solution)/shard_map/scatter-add | solution.py:76
  1286.8 14.4 %fusion.29 = f32[16,8,8,128]{3,2,1,0:T(8,128)} fusion(f32[16,8,8,128]{3,2,1,0:T(8,128)} %scatter-add.131, f32[16,8,8,128]{3,2,1,0:T(8,128)S(1)} %fusion.81, f32[16,6,8,128]{3,2,1,0:T(8,128)} %copy-done.10, f32[16,6,8,128]{3,2,1,0:T(8,128)S(1)} %collective-permute-done.24, f32[16,20,20,6]{3,2,1,0:T(8,128)} %copy.163, f32[16,20,6,128]{3,2,1,0:T(8,128)S(1)} %copy.155, ...), kind=kLoop, calls=%fused_computation.129 | loop fusion | flops 16252928 | bytes 11481088 | tf_op jit(solution)/shard_map/sub | solution.py:130
  1303.7 104.6 %psum.7 = f32[16,16]{1,0:T(8,128)S(1)} all-reduce(f32[16,16]{1,0:T(8,128)S(1)} %convolution_bitcast_fusion), channel_id=1, replica_groups=mesh['slab'=4,'row'=8,'col'=8] {'slab','row','col'}, use_global_device_ids=true, to_apply=%region_8.10 | all-reduce | flops 256 | bytes 2048 | tf_op jit(solution)/shard_map/psum | solution.py:133
  (238 shorter events, 279.8 us)
Async XLA Ops:
  0.6 9.0 copy-start
  0.6 13.0 copy-start.9
  1.9 11.7 collective-permute-start.1
  5.9 11.6 collective-permute-start
  10.5 170.5 %copy-start.14 = (f32[8,384]{1,0:T(8,128)}, f32[8,384]{1,0:T(8,128)S(1)}, u32[]{:S(2)}) copy-start(f32[8,384]{1,0:T(8,128)S(1)} %fusion.180) | copy-start | bytes 36868
  10.5 171.0 %copy-start.19 = (f32[3072]{0:T(1024)}, f32[3072]{0:T(1024)S(1)}, u32[]{:S(2)}) copy-start(f32[3072]{0:T(1024)S(1)} %mul.295) | copy-start | bytes 36868
  13.8 3.7 copy-start.8
  18.8 12.0 copy-start.24
  18.8 12.0 copy-start.25
  19.4 31.6 %collective-permute-start.2 = (f32[16,20,6,128]{3,0,2,1:T(8,128)S(1)}, f32[16,20,6,128]{3,0,2,1:T(8,128)S(1)}, u32[]{:S(2)}, u32[]{:S(2)}) collective-permute-start(f32[16,20,6,128]{3,0,2,1:T(8,128)S(1)} %copy.109), channel_id=1, source_target_pairs={{8,0},{16,8},{24,16},{32,24},{40,32},{48,40},{56,48},{9,1},{17,9},... | collective-permute-start | bytes 2949128 | tf_op jit(solution)/shard_map/ppermute | solution.py:27
  21.2 32.4 %collective-permute-start.3 = (f32[16,20,6,128]{3,0,2,1:T(8,128)S(1)}, f32[16,20,6,128]{3,0,2,1:T(8,128)S(1)}, u32[]{:S(2)}, u32[]{:S(2)}) collective-permute-start(f32[16,20,6,128]{3,0,2,1:T(8,128)S(1)} %copy.111), channel_id=1, source_target_pairs={{0,8},{8,16},{16,24},{24,32},{32,40},{40,48},{48,56},{1,9},{9,17},... | collective-permute-start | bytes 2949128 | tf_op jit(solution)/shard_map/ppermute | solution.py:24
  30.9 127.4 %copy-start.22 = (s32[3072]{0:T(1024)}, s32[3072]{0:T(1024)S(1)}, u32[]{:S(2)}) copy-start(s32[3072]{0:T(1024)S(1)} %fusion.179) | copy-start | bytes 36868
  30.9 152.2 %copy-start.23 = (s32[3072,1]{0,1:T(1,128)}, s32[3072,1]{0,1:T(1,128)S(1)}, u32[]{:S(2)}) copy-start(s32[3072,1]{0,1:T(1,128)S(1)} %compare_select_fusion) | copy-start | bytes 36868
  65.0 40.9 %collective-permute-start.4 = (f32[16,20,20,6]{2,0,3,1:T(8,128)}, f32[16,20,20,6]{2,0,3,1:T(8,128)}, u32[]{:S(2)}, u32[]{:S(2)}) collective-permute-start(f32[16,20,20,6]{2,0,3,1:T(8,128)} %copy.115), channel_id=1, source_target_pairs={{1,0},{2,1},{3,2},{4,3},{5,4},{6,5},{7,6},{9,8},{10,9},{11,10},{12... | collective-permute-start | bytes 460808 | tf_op jit(solution)/shard_map/ppermute | solution.py:27
  75.0 47.7 %collective-permute-start.5 = (f32[16,20,20,6]{2,0,3,1:T(8,128)}, f32[16,20,20,6]{2,0,3,1:T(8,128)}, u32[]{:S(2)}, u32[]{:S(2)}) collective-permute-start(f32[16,20,20,6]{2,0,3,1:T(8,128)} %copy.117), channel_id=1, source_target_pairs={{0,1},{1,2},{2,3},{3,4},{4,5},{5,6},{6,7},{8,9},{9,10},{10,11},{11... | collective-permute-start | bytes 460808 | tf_op jit(solution)/shard_map/ppermute | solution.py:24
  235.4 28.8 %slice-start = ((s8[7864320]{0:T(1024)(128)(4,1)}), s8[3670016]{0:T(1024)(128)(4,1)S(1)}, s32[]{:S(2)}) async-start(s8[7864320]{0:T(1024)(128)(4,1)} %bitcast.44), calls=%async_computation | async-start | bytes 7340032
  238.3 26.0 %slice-start.1 = ((s8[7864320]{0:T(1024)(128)(4,1)}), s8[4194304]{0:T(1024)(128)(4,1)S(1)}, s32[]{:S(2)}) async-start(s8[7864320]{0:T(1024)(128)(4,1)} %bitcast.44), calls=%async_computation.1 | async-start | bytes 8388608
  239.4 24.8 %collective-permute-start.6 = (f32[16,6,20,140]{3,0,2,1:T(8,128)S(1)}, f32[16,6,20,140]{3,0,2,1:T(8,128)S(1)}, u32[]{:S(2)}, u32[]{:S(2)}) collective-permute-start(f32[16,6,20,140]{3,0,2,1:T(8,128)S(1)} %copy.124), channel_id=1, source_target_pairs={{0,64},{64,128},{128,192},{1,65},{65,129},{129,193},{2,66},{66,130... | collective-permute-start | bytes 3225608 | tf_op jit(solution)/shard_map/ppermute | solution.py:24
  243.9 20.3 %slice-start.2 = ((f32[16,20,20,140]{3,2,1,0:T(8,128)}), f32[16,8,20,140]{3,2,1,0:T(8,128)S(1)}, s32[]{:S(2)}) async-start(f32[16,20,20,140]{3,2,1,0:T(8,128)} %reshape.788), calls=%async_computation.2 | async-start | bytes 6291456 | tf_op jit(solution)/shard_map/slice | solution.py:68
  244.0 25.6 %collective-permute-start.7 = (f32[16,6,20,140]{3,0,2,1:T(8,128)S(1)}, f32[16,6,20,140]{3,0,2,1:T(8,128)S(1)}, u32[]{:S(2)}, u32[]{:S(2)}) collective-permute-start(f32[16,6,20,140]{3,0,2,1:T(8,128)S(1)} %copy.126), channel_id=1, source_target_pairs={{64,0},{128,64},{192,128},{65,1},{129,65},{193,129},{66,2},{130,66... | collective-permute-start | bytes 3225608 | tf_op jit(solution)/shard_map/ppermute | solution.py:27
  271.9 33.5 %collective-permute-start.8 = (f32[16,8,6,140]{3,1,2,0:T(8,128)S(1)}, f32[16,8,6,140]{3,1,2,0:T(8,128)S(1)}, u32[]{:S(2)}, u32[]{:S(2)}) collective-permute-start(f32[16,8,6,140]{3,1,2,0:T(8,128)S(1)} %copy.128), channel_id=1, source_target_pairs={{0,8},{8,16},{16,24},{24,32},{32,40},{40,48},{48,56},{1,9},{9,17},... | collective-permute-start | bytes 1290248 | tf_op jit(solution)/shard_map/ppermute | solution.py:24
  297.0 67.4 %collective-permute-start.9 = (f32[16,8,6,140]{3,1,2,0:T(8,128)S(1)}, f32[16,8,6,140]{3,1,2,0:T(8,128)}, u32[]{:S(2)}, u32[]{:S(2)}) collective-permute-start(f32[16,8,6,140]{3,1,2,0:T(8,128)S(1)} %copy.130), channel_id=1, source_target_pairs={{8,0},{16,8},{24,16},{32,24},{40,32},{48,40},{56,48},{9,1},{17,9},... | collective-permute-start | bytes 1290248 | tf_op jit(solution)/shard_map/ppermute | solution.py:27
  373.6 19.6 %copy-start.4 = (f32[16,8,8,140]{3,2,1,0:T(8,128)S(1)}, f32[16,8,8,140]{3,2,1,0:T(8,128)}, u32[]{:S(2)}) copy-start(f32[16,8,8,140]{3,2,1,0:T(8,128)} %scatter-add.86) | copy-start | bytes 1720324
  375.9 17.4 %collective-permute-start.10 = (f32[16,8,8,6]{3,2,1,0:T(8,128)S(1)}, f32[16,8,8,6]{3,2,1,0:T(8,128)S(1)}, u32[]{:S(2)}, u32[]{:S(2)}) collective-permute-start(f32[16,8,8,6]{3,2,1,0:T(8,128)S(1)} %get-tuple-element.254), channel_id=1, source_target_pairs={{0,1},{1,2},{2,3},{3,4},{4,5},{5,6},{6,7},{8,9},{9,10},{10,11},{11... | collective-permute-start | bytes 73736 | tf_op jit(solution)/shard_map/ppermute | solution.py:24
  388.5 35.0 %copy-start.17 = (f32[8,8,128]{2,1,0:T(8,128)S(1)}, f32[8,8,128]{2,1,0:T(8,128)}, u32[]{:S(2)}) copy-start(f32[8,8,128]{2,1,0:T(8,128)} %param.47) | copy-start | bytes 98308
  388.6 10.8 collective-permute-start.11
  439.4 392.1 %copy-start.2 = (f32[16,8,8,128]{3,2,1,0:T(8,128)}, f32[16,8,8,128]{3,2,1,0:T(8,128)S(1)}, u32[]{:S(2)}) copy-start(f32[16,8,8,128]{3,2,1,0:T(8,128)S(1)} %get-tuple-element.219) | copy-start | bytes 1572868
  439.5 8.5 collective-permute-start.12
  440.8 8.7 collective-permute-start.13
  449.5 41.2 %copy-start.11 = (f32[16,6,8,128]{3,2,1,0:T(8,128)}, f32[16,6,8,128]{3,2,1,0:T(8,128)S(1)}, u32[]{:S(2)}) copy-start(f32[16,6,8,128]{3,2,1,0:T(8,128)S(1)} %collective-permute-done.13) | copy-start | bytes 1179652
  450.5 39.6 %collective-permute-start.14 = (f32[16,20,6,128]{3,0,2,1:T(8,128)S(1)}, f32[16,20,6,128]{3,0,2,1:T(8,128)S(1)}, u32[]{:S(2)}, u32[]{:S(2)}) collective-permute-start(f32[16,20,6,128]{3,0,2,1:T(8,128)S(1)} %copy.132), channel_id=1, source_target_pairs={{8,0},{16,8},{24,16},{32,24},{40,32},{48,40},{56,48},{9,1},{17,9},... | collective-permute-start | bytes 2949128 | tf_op jit(solution)/shard_map/ppermute | solution.py:27
  452.3 38.0 %collective-permute-start.15 = (f32[16,20,6,128]{3,0,2,1:T(8,128)S(1)}, f32[16,20,6,128]{3,0,2,1:T(8,128)S(1)}, u32[]{:S(2)}, u32[]{:S(2)}) collective-permute-start(f32[16,20,6,128]{3,0,2,1:T(8,128)S(1)} %copy.134), channel_id=1, source_target_pairs={{0,8},{8,16},{16,24},{24,32},{32,40},{40,48},{48,56},{1,9},{9,17},... | collective-permute-start | bytes 2949128 | tf_op jit(solution)/shard_map/ppermute | solution.py:24
  500.5 36.1 %collective-permute-start.16 = (f32[16,20,20,6]{2,0,3,1:T(8,128)}, f32[16,20,20,6]{2,0,3,1:T(8,128)}, u32[]{:S(2)}, u32[]{:S(2)}) collective-permute-start(f32[16,20,20,6]{2,0,3,1:T(8,128)} %copy.138), channel_id=1, source_target_pairs={{1,0},{2,1},{3,2},{4,3},{5,4},{6,5},{7,6},{9,8},{10,9},{11,10},{12... | collective-permute-start | bytes 460808 | tf_op jit(solution)/shard_map/ppermute | solution.py:27
  507.1 53.1 %collective-permute-start.17 = (f32[16,20,20,6]{2,0,3,1:T(8,128)}, f32[16,20,20,6]{2,0,3,1:T(8,128)}, u32[]{:S(2)}, u32[]{:S(2)}) collective-permute-start(f32[16,20,20,6]{2,0,3,1:T(8,128)} %copy.140), channel_id=1, source_target_pairs={{0,1},{1,2},{2,3},{3,4},{4,5},{5,6},{6,7},{8,9},{9,10},{10,11},{11... | collective-permute-start | bytes 460808 | tf_op jit(solution)/shard_map/ppermute | solution.py:24
  617.6 3.3 copy-start.20
  674.5 29.8 %slice-start.3 = ((s8[7864320]{0:T(1024)(128)(4,1)}), s8[3670016]{0:T(1024)(128)(4,1)S(1)}, s32[]{:S(2)}) async-start(s8[7864320]{0:T(1024)(128)(4,1)} %bitcast.46), calls=%async_computation.3 | async-start | bytes 7340032
  677.4 27.0 %slice-start.4 = ((s8[7864320]{0:T(1024)(128)(4,1)}), s8[4194304]{0:T(1024)(128)(4,1)S(1)}, s32[]{:S(2)}) async-start(s8[7864320]{0:T(1024)(128)(4,1)} %bitcast.46), calls=%async_computation.4 | async-start | bytes 8388608
  678.5 25.8 %collective-permute-start.18 = (f32[16,6,20,140]{3,0,2,1:T(8,128)S(1)}, f32[16,6,20,140]{3,0,2,1:T(8,128)S(1)}, u32[]{:S(2)}, u32[]{:S(2)}) collective-permute-start(f32[16,6,20,140]{3,0,2,1:T(8,128)S(1)} %copy.146), channel_id=1, source_target_pairs={{0,64},{64,128},{128,192},{1,65},{65,129},{129,193},{2,66},{66,130... | collective-permute-start | bytes 3225608 | tf_op jit(solution)/shard_map/ppermute | solution.py:24
  684.0 20.3 %slice-start.5 = ((f32[16,20,20,140]{3,2,1,0:T(8,128)}), f32[16,8,20,140]{3,2,1,0:T(8,128)S(1)}, s32[]{:S(2)}) async-start(f32[16,20,20,140]{3,2,1,0:T(8,128)} %reshape.791), calls=%async_computation.5 | async-start | bytes 6291456 | tf_op jit(solution)/shard_map/slice | solution.py:68
  684.1 25.6 %collective-permute-start.19 = (f32[16,6,20,140]{3,0,2,1:T(8,128)S(1)}, f32[16,6,20,140]{3,0,2,1:T(8,128)S(1)}, u32[]{:S(2)}, u32[]{:S(2)}) collective-permute-start(f32[16,6,20,140]{3,0,2,1:T(8,128)S(1)} %copy.148), channel_id=1, source_target_pairs={{64,0},{128,64},{192,128},{65,1},{129,65},{193,129},{66,2},{130,66... | collective-permute-start | bytes 3225608 | tf_op jit(solution)/shard_map/ppermute | solution.py:27
  711.8 20.4 %copy-start.18 = (f32[8,8,128]{2,1,0:T(8,128)S(1)}, f32[8,8,128]{2,1,0:T(8,128)}, u32[]{:S(2)}) copy-start(f32[8,8,128]{2,1,0:T(8,128)} %param.47) | copy-start | bytes 98308
  712.0 26.2 %collective-permute-start.20 = (f32[16,8,6,140]{3,1,2,0:T(8,128)S(1)}, f32[16,8,6,140]{3,1,2,0:T(8,128)S(1)}, u32[]{:S(2)}, u32[]{:S(2)}) collective-permute-start(f32[16,8,6,140]{3,1,2,0:T(8,128)S(1)} %copy.150), channel_id=1, source_target_pairs={{0,8},{8,16},{16,24},{24,32},{32,40},{40,48},{48,56},{1,9},{9,17},... | collective-permute-start | bytes 1290248 | tf_op jit(solution)/shard_map/ppermute | solution.py:24
  730.9 72.7 %collective-permute-start.21 = (f32[16,8,6,140]{3,1,2,0:T(8,128)}, f32[16,8,6,140]{3,1,2,0:T(8,128)}, u32[]{:S(2)}, u32[]{:S(2)}) collective-permute-start(f32[16,8,6,140]{3,1,2,0:T(8,128)} %copy.152), channel_id=1, source_target_pairs={{8,0},{16,8},{24,16},{32,24},{40,32},{48,40},{56,48},{9,1},{17,9},... | collective-permute-start | bytes 1290248 | tf_op jit(solution)/shard_map/ppermute | solution.py:27
  815.0 20.6 %copy-start.5 = (f32[16,8,8,140]{3,2,1,0:T(8,128)S(1)}, f32[16,8,8,140]{3,2,1,0:T(8,128)}, u32[]{:S(2)}) copy-start(f32[16,8,8,140]{3,2,1,0:T(8,128)} %scatter-add.99) | copy-start | bytes 1720324
  815.0 22.7 %collective-permute-start.22 = (f32[16,8,8,6]{3,2,1,0:T(8,128)S(1)}, f32[16,8,8,6]{3,2,1,0:T(8,128)S(1)}, u32[]{:S(2)}, u32[]{:S(2)}) collective-permute-start(f32[16,8,8,6]{3,2,1,0:T(8,128)S(1)} %get-tuple-element.252), channel_id=1, source_target_pairs={{0,1},{1,2},{2,3},{3,4},{4,5},{5,6},{6,7},{8,9},{9,10},{10,11},{11... | collective-permute-start | bytes 73736 | tf_op jit(solution)/shard_map/ppermute | solution.py:24
  835.8 10.8 collective-permute-start.23
  888.0 8.5 collective-permute-start.24
  889.3 8.7 collective-permute-start.25
  898.0 31.1 %copy-start.10 = (f32[16,6,8,128]{3,2,1,0:T(8,128)}, f32[16,6,8,128]{3,2,1,0:T(8,128)S(1)}, u32[]{:S(2)}) copy-start(f32[16,6,8,128]{3,2,1,0:T(8,128)S(1)} %collective-permute-done.25) | copy-start | bytes 1179652
  899.0 29.5 %collective-permute-start.26 = (f32[16,20,6,128]{3,0,2,1:T(8,128)S(1)}, f32[16,20,6,128]{3,0,2,1:T(8,128)S(1)}, u32[]{:S(2)}, u32[]{:S(2)}) collective-permute-start(f32[16,20,6,128]{3,0,2,1:T(8,128)S(1)} %copy.154), channel_id=1, source_target_pairs={{8,0},{16,8},{24,16},{32,24},{40,32},{48,40},{56,48},{9,1},{17,9},... | collective-permute-start | bytes 2949128 | tf_op jit(solution)/shard_map/ppermute | solution.py:27
  900.9 27.9 %collective-permute-start.27 = (f32[16,20,6,128]{3,0,2,1:T(8,128)S(1)}, f32[16,20,6,128]{3,0,2,1:T(8,128)S(1)}, u32[]{:S(2)}, u32[]{:S(2)}) collective-permute-start(f32[16,20,6,128]{3,0,2,1:T(8,128)S(1)} %copy.156), channel_id=1, source_target_pairs={{0,8},{8,16},{16,24},{24,32},{32,40},{40,48},{48,56},{1,9},{9,17},... | collective-permute-start | bytes 2949128 | tf_op jit(solution)/shard_map/ppermute | solution.py:24
  939.0 19.4 %collective-permute-start.28 = (f32[16,20,20,6]{2,0,3,1:T(8,128)}, f32[16,20,20,6]{2,0,3,1:T(8,128)}, u32[]{:S(2)}, u32[]{:S(2)}) collective-permute-start(f32[16,20,20,6]{2,0,3,1:T(8,128)} %copy.160), channel_id=1, source_target_pairs={{1,0},{2,1},{3,2},{4,3},{5,4},{6,5},{7,6},{9,8},{10,9},{11,10},{12... | collective-permute-start | bytes 460808 | tf_op jit(solution)/shard_map/ppermute | solution.py:27
  945.6 17.3 %collective-permute-start.29 = (f32[16,20,20,6]{2,0,3,1:T(8,128)}, f32[16,20,20,6]{2,0,3,1:T(8,128)}, u32[]{:S(2)}, u32[]{:S(2)}) collective-permute-start(f32[16,20,20,6]{2,0,3,1:T(8,128)} %copy.162), channel_id=1, source_target_pairs={{0,1},{1,2},{2,3},{3,4},{4,5},{5,6},{6,7},{8,9},{9,10},{10,11},{11... | collective-permute-start | bytes 460808 | tf_op jit(solution)/shard_map/ppermute | solution.py:24
  1077.2 41.8 %slice-start.6 = ((s8[7864320]{0:T(1024)(128)(4,1)}), s8[3670016]{0:T(1024)(128)(4,1)S(1)}, s32[]{:S(2)}) async-start(s8[7864320]{0:T(1024)(128)(4,1)} %bitcast.48), calls=%async_computation.6 | async-start | bytes 7340032
  1080.0 38.9 %slice-start.7 = ((s8[7864320]{0:T(1024)(128)(4,1)}), s8[4194304]{0:T(1024)(128)(4,1)S(1)}, s32[]{:S(2)}) async-start(s8[7864320]{0:T(1024)(128)(4,1)} %bitcast.48), calls=%async_computation.7 | async-start | bytes 8388608
  1081.2 37.7 %collective-permute-start.30 = (f32[16,6,20,140]{3,0,2,1:T(8,128)S(1)}, f32[16,6,20,140]{3,0,2,1:T(8,128)S(1)}, u32[]{:S(2)}, u32[]{:S(2)}) collective-permute-start(f32[16,6,20,140]{3,0,2,1:T(8,128)S(1)} %copy.168), channel_id=1, source_target_pairs={{0,64},{64,128},{128,192},{1,65},{65,129},{129,193},{2,66},{66,130... | collective-permute-start | bytes 3225608 | tf_op jit(solution)/shard_map/ppermute | solution.py:24
  1086.7 32.2 %slice-start.8 = ((f32[16,20,20,140]{3,2,1,0:T(8,128)}), f32[16,8,20,140]{3,2,1,0:T(8,128)S(1)}, s32[]{:S(2)}) async-start(f32[16,20,20,140]{3,2,1,0:T(8,128)} %reshape.794), calls=%async_computation.8 | async-start | bytes 6291456 | tf_op jit(solution)/shard_map/slice | solution.py:68
  1086.7 37.8 %collective-permute-start.31 = (f32[16,6,20,140]{3,0,2,1:T(8,128)S(1)}, f32[16,6,20,140]{3,0,2,1:T(8,128)S(1)}, u32[]{:S(2)}, u32[]{:S(2)}) collective-permute-start(f32[16,6,20,140]{3,0,2,1:T(8,128)S(1)} %copy.170), channel_id=1, source_target_pairs={{64,0},{128,64},{192,128},{65,1},{129,65},{193,129},{66,2},{130,66... | collective-permute-start | bytes 3225608 | tf_op jit(solution)/shard_map/ppermute | solution.py:27
  1126.9 49.3 %collective-permute-start.32 = (f32[16,8,6,140]{3,1,2,0:T(8,128)S(1)}, f32[16,8,6,140]{3,1,2,0:T(8,128)S(1)}, u32[]{:S(2)}, u32[]{:S(2)}) collective-permute-start(f32[16,8,6,140]{3,1,2,0:T(8,128)S(1)} %copy.172), channel_id=1, source_target_pairs={{0,8},{8,16},{16,24},{24,32},{32,40},{40,48},{48,56},{1,9},{9,17},... | collective-permute-start | bytes 1290248 | tf_op jit(solution)/shard_map/ppermute | solution.py:24
  1166.7 50.4 %collective-permute-start.33 = (f32[16,8,6,140]{3,1,2,0:T(8,128)}, f32[16,8,6,140]{3,1,2,0:T(8,128)}, u32[]{:S(2)}, u32[]{:S(2)}) collective-permute-start(f32[16,8,6,140]{3,1,2,0:T(8,128)} %copy.174), channel_id=1, source_target_pairs={{8,0},{16,8},{24,16},{32,24},{40,32},{48,40},{56,48},{9,1},{17,9},... | collective-permute-start | bytes 1290248 | tf_op jit(solution)/shard_map/ppermute | solution.py:27
  1228.5 6.2 copy-start.6
  1228.5 11.9 collective-permute-start.34
  1235.7 27.6 %collective-permute-start.35 = (f32[16,8,8,6]{3,2,1,0:T(8,128)}, f32[16,8,8,6]{3,2,1,0:T(8,128)}, u32[]{:S(2)}, u32[]{:S(2)}) collective-permute-start(f32[16,8,8,6]{3,2,1,0:T(8,128)} %get-tuple-element.249), channel_id=1, source_target_pairs={{1,0},{2,1},{3,2},{4,3},{5,4},{6,5},{7,6},{9,8},{10,9},{11,10},{12... | collective-permute-start | bytes 73736 | tf_op jit(solution)/shard_map/ppermute | solution.py:27
  1286.8 122.0 %copy-start.1 = (f32[4,384]{1,0:T(4,128)S(1)}, f32[4,384]{1,0:T(4,128)}, u32[]{:S(2)}) copy-start(f32[4,384]{1,0:T(4,128)} %param.52) | copy-start | bytes 18436
  (7 other events, 12.4 us)
where the time goes:
time: 1420 us; the launch traced here: 1410 us
  local copies, waits for them, and re-layouts  426 us (30%)
  waiting for transfers between devices  394 us (28%)
  starting transfers between devices  258 us (18%)
  other arithmetic  221 us (16%)
  blocking collectives  105 us (7%)
    ppermute x18, waiting for transfers between devices, padded_2(): lax.ppermute(lax.slice_in_dim(block, 0, width, axis=dim), axis, backward)  264 us
    ppermute x18, starting transfers between devices, padded_2(): lax.ppermute(lax.slice_in_dim(block, block.shape[dim] - width, None, axis...  226 us
    ppermute x18, waiting for transfers between devices, padded_2(): lax.ppermute(lax.slice_in_dim(block, block.shape[dim] - width, None, axis...  130 us
    psum x1, blocking collectives, shards(): summed_gram = lax.psum(partial_gram, ('slab', 'row', 'col'))  105 us
    scatter-add x6, local copies, waits for them, and re-layouts, add_rims(): return inner.at[tuple(trailing)].add(upper_part)  83.2 us
    scatter-add x3, other arithmetic, spread_rims(): accumulated = jnp.zeros((bands, wide_x * wide_y * wide_z), jnp.float32).a...  81.8 us
    reshape x6, local copies, waits for them, and re-layouts, filter_step(): padded.reshape(bands, -1)  63 us
    gather x3, local copies, waits for them, and re-layouts, filter_step(): jnp.take(padded.reshape(bands, -1), ext_index, axis=1)  61.9 us
  transfers between devices with their start and end apart: 36, of which 32 were waited for; matrix products, arithmetic and copies ran while one was open for 7% of the time, Pallas kernels for 0%

commit v1 on v0

v1 whole, which is shorter than its diff:
```python
import jax
import jax.numpy as jnp
from jax import lax
from jax.experimental import pallas as pl
from jax.experimental.pallas import tpu as pltpu
from jax.sharding import PartitionSpec as P

stencil_weights = (
    -5369.0 / 1800.0,
    12.0 / 7.0,
    -15.0 / 56.0,
    10.0 / 189.0,
    -1.0 / 112.0,
    2.0 / 1925.0,
    -1.0 / 16632.0,
)
lower_edge = 3.0
upper_edge = 17.0
centre = 0.5 * (upper_edge + lower_edge)
half_width = 0.5 * (upper_edge - lower_edge)

BANDS = 16
GX, GY, LANES = 32, 64, 128
PX, PY = 6, 8
PITCH = GY + 2 * PY
ROWS = (GX + 2 * PX) * PITCH
TILES = 12
BLOCKS = 32
SLOTS = 8
CAP = 2 * BLOCKS * SLOTS
HALO_ROWS = BLOCKS * 4 * 8 + BLOCKS
FAR = -4096
VMEM = pl.BlockSpec(memory_space=pltpu.VMEM)
SMEM = pl.BlockSpec(memory_space=pltpu.SMEM)
HIGHEST = lax.Precision.HIGHEST


def lane_of(shape):
    return lax.broadcasted_iota(jnp.int32, shape, len(shape) - 1)


def row_of(shape):
    return lax.broadcasted_iota(jnp.int32, shape, len(shape) - 2)


def pack_kernel(place, positions, species, counts, wave, potential, out):
    col = place[2]
    low = lane_of((8, LANES)) < 64
    lane = lane_of((8, LANES))
    info = jnp.zeros((8, LANES), jnp.int32)
    for slot in range(SLOTS):
        live = slot < counts[0]
        base = (positions[0, slot] + PX) * PITCH + positions[1, slot] + PY
        z = jnp.where(live, positions[2, slot], FAR)
        info = jnp.where(lane == slot, z, info)
        info = jnp.where(lane == SLOTS + slot, base * 4 + species[slot], info)
    info = info.astype(jnp.float32)

    def halves(tile, other):
        return (
            jnp.where(low, tile, pltpu.roll(other, 64, 1)),
            jnp.where(low, pltpu.roll(tile, 64, 1), other),
        )

    fixed = [halves(potential[k], potential[k + 4]) for k in range(4)]
    for pair in range(2):
        slabs = [lax.rem(2 * pair + h + col, 4) for h in range(2)]

        def one(r, carry):
            band = pair * 8 + r
            for k in range(4):
                parts = halves(wave[band, k], wave[band, k + 4])
                for h in range(2):
                    dest = slabs[h] * 8 + r
                    out[dest, k] = parts[h]
                    out[dest, 4 + k] = fixed[k][h]
            for h in range(2):
                out[slabs[h] * 8 + r, 8] = info
            return carry

        lax.fori_loop(0, 8, one, 0)


def edge_kernel(held, low_out, high_out):
    even = (lane_of((8, LANES)) & 32) == 0

    def one(d, carry):
        for field in range(2):
            for pair in range(2):
                first = held[d, field * 4 + 2 * pair]
                second = held[d, field * 4 + 2 * pair + 1]
                at = pl.multiple_of(d * 32, 32) + field * 16 + pair * 8
                low_out[pl.ds(at, 8), :] = jnp.where(even, first, pltpu.roll(second, 32, 1))
                high_out[pl.ds(at, 8), :] = jnp.where(even, pltpu.roll(first, 96, 1), second)
        return carry

    lax.fori_loop(0, BLOCKS, one, 0)
    rows = held[:, 8, 0, :]
    low_out[BLOCKS * 32 :, :] = rows
    high_out[BLOCKS * 32 :, :] = rows


def sphere_kernel(offsets, beta, out):
    points = beta.shape[1]
    for kind in range(beta.shape[0]):
        dx = offsets[3 * kind : 3 * kind + 1, :]
        dy = offsets[3 * kind + 1 : 3 * kind + 2, :]
        dz = offsets[3 * kind + 2 : 3 * kind + 3, :]
        row = 16 + (dx + 3) * 8 + dy + 4
        row = jnp.where(jnp.abs(dx) == 4, jnp.where(dx > 0, 8, 0) + dy + 3, row)
        row = jnp.where(dy == 4, 72 + dx + 3, row)
        row = jnp.where(jnp.abs(dy) == 5, jnp.where(dy > 0, 81, 80), row)
        row = jnp.where(jnp.abs(dx) == 5, jnp.where(dx > 0, 89, 88), row)
        left = (row_of((TILES * 8, points)) == row).astype(jnp.float32)
        right = jnp.where(row_of((LANES, points)) == dz + 5, beta[kind : kind + 1, :], 0.0)
        out[kind] = lax.dot_general(
            left,
            right,
            (((1,), (1,)), ((), ())),
            precision=HIGHEST,
            preferred_element_type=jnp.float32,
        )


def tile_refs(ref, base):
    yield ref.at[pl.ds(base - 4 * PITCH - 3, 8), :]
    yield ref.at[pl.ds(base + 4 * PITCH - 3, 8), :]
    for dx in range(-3, 4):
        yield ref.at[pl.ds(base + dx * PITCH - 4, 8), :]
    yield ref.at[pl.ds(base - 3 * PITCH + 4, 8, stride=PITCH), :]
    yield ref.at[pl.ds(base - 5, 2, stride=10), :]
    yield ref.at[pl.ds(base - 5 * PITCH, 2, stride=10 * PITCH), :]


TILE_ROWS = (8,) * 10 + (2, 2)


def filter_kernel(
    place,
    coupling,
    held,
    low_in,
    high_in,
    sphere,
    out,
    buf_a,
    buf_b,
    pot,
    zpart,
    rolled,
    acc,
    total,
    table_v,
    table,
    listed,
    extra,
    sem,
):
    slab, col = place[0], place[2]
    half = lax.rem(slab + 4 - lax.rem(col, 4), 4) % 2
    depth = col * 2 + half
    lane8 = lane_of((8, LANES))

    own = held[:, 8, 0, :]
    outer = jnp.where(half == 0, low_in[BLOCKS * 32 :, :], high_in[BLOCKS * 32 :, :])
    rows = jnp.concatenate([own, outer], axis=0).astype(jnp.int32)
    moved = pltpu.roll(rows, LANES - SLOTS, 1)
    lane_z = rows - (depth * 64 - 32)
    kind = jnp.where((lane_z >= 7) & (lane_z < 121), 1, 0)
    kind = kind + jnp.where((lane_z >= 17) & (lane_z < 111), 1, 0)
    kind = kind + jnp.where((lane_z >= 27) & (lane_z < 101), 1, 0)
    kind = jnp.where(moved > 0, kind, 0)
    table_v[...] = jnp.where(kind > 0, moved * 512 + lane_z * 4 + kind, 0)
    copy = pltpu.make_async_copy(table_v, table, sem)
    copy.start()

    buf_a[...] = jnp.zeros_like(buf_a)
    buf_b[...] = jnp.zeros_like(buf_b)
    inner = (lane8 >= 32) & (lane8 < 96)

    def gather_block(d, carry):
        s, r = d // 8, lax.rem(d, 8)
        for x in range(8):
            high, k = x // 4, x % 4
            pair, m = k // 2, k % 2
            group = high * 2 + m
            for field in range(2):
                at = pl.multiple_of(d * 32, 32) + field * 16 + pair * 8
                mid = held[d, field * 4 + k]
                mid = pltpu.roll(mid, (32 - 64 * high) % LANES, 1)
                left = low_in[pl.ds(at, 8), :]
                right = high_in[pl.ds(at, 8), :]
                if group:
                    left = pltpu.roll(left, LANES - 32 * group, 1)
                if group != 3:
                    right = pltpu.roll(right, 96 - 32 * group, 1)
                tile = jnp.where(inner, mid, jnp.where(lane8 < 32, left, right))
                if field == 0:
                    at = pl.multiple_of((s * 8 + x + PX) * PITCH + PY + r * 8, 8)
                    buf_a[pl.ds(at, 8), :] = tile
                else:
                    at = pl.multiple_of((s * 8 + x) * GY + r * 8, 8)
                    pot[pl.ds(at, 8), :] = tile - centre
        return carry

    lax.fori_loop(0, BLOCKS, gather_block, 0)
    copy.wait()

    def sort_slot(i, carry):
        n3, n2, n1 = carry
        for slot in range(SLOTS):
            word = table[i, slot]
            kind = word & 3
            listed[n3] = word
            extra[n2] = word
            extra[CAP + n1] = word
            n3 = n3 + jnp.where(kind == 3, 1, 0)
            n2 = n2 + jnp.where(kind == 2, 1, 0)
            n1 = n1 + jnp.where(kind == 1, 1, 0)
        return n3, n2, n1

    zero = jnp.int32(0)
    n3, n2, n1 = lax.fori_loop(0, 2 * BLOCKS, sort_slot, (zero, zero, zero))

    def move_second(i, carry):
        listed[n3 + i] = extra[i]
        return carry

    def move_first(i, carry):
        listed[n3 + n2 + i] = extra[CAP + i]
        return carry

    lax.fori_loop(0, n2, move_second, 0)
    lax.fori_loop(0, n1, move_first, 0)

    apart = jnp.abs(lane_of((LANES, LANES)) - row_of((LANES, LANES)))
    band = jnp.zeros((LANES, LANES), jnp.float32)
    for reach in range(7):
        band = jnp.where(apart == reach, -0.5 * stencil_weights[reach], band)
    band_high = band.astype(jnp.bfloat16)
    band_low = (band - band_high.astype(jnp.float32)).astype(jnp.bfloat16)

    lanes = lane_of((1, LANES))
    inside = ((lanes >= 32) | (depth > 0)) & ((lanes < 96) | (depth < 15))
    mask = jnp.where(inside, 1.0, 0.0)

    def z_block(source):
        def one(x, carry):
            at = pl.multiple_of((x + PX) * PITCH + PY, 8)
            field = source[pl.ds(at, GY), :]
            high = field.astype(jnp.bfloat16)
            low = (field - high.astype(jnp.float32)).astype(jnp.bfloat16)
            part = jnp.dot(high, band_high, preferred_element_type=jnp.float32)
            part += jnp.dot(low, band_high, preferred_element_type=jnp.float32)
            part += jnp.dot(high, band_low, preferred_element_type=jnp.float32)
            zpart[pl.ds(pl.multiple_of(x * GY, GY), GY), :] = part
            return carry

        lax.fori_loop(0, GX, one, 0)

    def local_part(source, target, scale, subtract):
        z_block(source)
        cube = source.reshape(GX + 2 * PX, PITCH, LANES)

        def one(x, carry):
            at = pl.multiple_of((x + PX) * PITCH + PY, 8)
            own_at = pl.multiple_of(x * GY, GY)
            field = source[pl.ds(at, GY), :]
            result = zpart[pl.ds(own_at, GY), :] + pot[pl.ds(own_at, GY), :] * field
            result += (-1.0 * stencil_weights[0]) * field
            for reach in range(1, 7):
                near = cube[x + PX, pl.ds(PY - reach, GY), :] + cube[x + PX, pl.ds(PY + reach, GY), :]
                near += source[pl.ds(at - reach * PITCH, GY), :]
                near += source[pl.ds(at + reach * PITCH, GY), :]
                result += (-0.5 * stencil_weights[reach]) * near
            result = result * scale
            if subtract:
                result -= target[pl.ds(at, GY), :]
            target[pl.ds(at, GY), :] = result
            return carry

        lax.fori_loop(0, GX, one, 0)

    def gather_atoms(source, count, first):
        def one(j, carry):
            word = listed[j]
            base = word >> 11
            kind = (word >> 9) & 3
            shift = ((word >> 2) & 127) - 5
            weight = coupling[kind]
            parts = []
            small = []
            for t, ref in enumerate(tile_refs(source, base)):
                size = TILE_ROWS[t]
                if first:
                    shape = sphere[kind, 8 * t : 8 * t + size, :]
                    shape = pltpu.roll(shape, shift, 1)
                    rolled[j, 8 * t : 8 * t + size, :] = shape
                else:
                    shape = rolled[j, 8 * t : 8 * t + size, :]
                product = ref[...] * shape
                (parts if size == 8 else small).append(product)
            while len(parts) > 1:
                parts = [a + b for a, b in zip(parts[::2], parts[1::2])] + ([parts[-1]] if len(parts) % 2 else [])
            acc[j] = parts[0] * weight
            acc[j, 0:2, :] += (small[0] + small[1]) * weight
            return carry

        lax.fori_loop(0, count, one, 0)

    def sum_atoms(count, scale):
        def one(i, carry):
            at = pl.multiple_of(i * 32, 32)
            part = jnp.sum(acc[pl.ds(at, 32)], axis=1)
            part = jnp.sum(part, axis=1, keepdims=True) * scale
            total[pl.ds(at, 32), :] = jnp.broadcast_to(part, (32, LANES))
            return carry

        lax.fori_loop(0, (count + 31) // 32, one, 0)

    def spread_atoms(target, count):
        def one(j, carry):
            base = listed[j] >> 11
            q = total[pl.ds(j, 1), :]
            refs = list(tile_refs(target, base))
            values = []
            for t, ref in enumerate(refs):
                size = TILE_ROWS[t]
                values.append(ref[...] + q * rolled[j, 8 * t : 8 * t + size, :])
            for ref, value in zip(refs, values):
                ref[...] = value
            return carry

        lax.fori_loop(0, count, one, 0)

    def clean(target):
        edge = PX * PITCH
        target[0:edge, :] = jnp.zeros((edge, LANES), jnp.float32)
        target[ROWS - edge :, :] = jnp.zeros((edge, LANES), jnp.float32)

        def one(x, carry):
            at = pl.multiple_of((x + PX) * PITCH, 8)
            target[pl.ds(at, PY), :] = jnp.zeros((PY, LANES), jnp.float32)
            target[pl.ds(at + PY + GY, PY), :] = jnp.zeros((PY, LANES), jnp.float32)
            target[pl.ds(at + PY, GY), :] = target[pl.ds(at + PY, GY), :] * mask
            return carry

        lax.fori_loop(0, GX, one, 0)

    def step(source, target, scale, subtract, count, first):
        gather_atoms(source, count, first)
        sum_atoms(count, scale)
        local_part(source, target, scale, subtract)
        spread_atoms(target, count)

    step(buf_a, buf_b, 1.0 / half_width, False, n3 + n2 + n1, True)
    clean(buf_b)
    step(buf_b, buf_a, 2.0 / half_width, True, n3 + n2, False)
    clean(buf_a)
    step(buf_a, buf_b, 2.0 / half_width, True, n3, False)

    low = lane8 < 64

    def send_block(d, carry):
        s, r = d // 8, lax.rem(d, 8)
        for k in range(4):
            at = pl.multiple_of((s * 8 + k + PX) * PITCH + PY + r * 8, 8)
            first = buf_b[pl.ds(at, 8), :]
            second = buf_b[pl.ds(at + 4 * PITCH, 8), :]
            out[d, k] = jnp.where(low, pltpu.roll(first, 96, 1), pltpu.roll(second, 32, 1))
        return carry

    lax.fori_loop(0, BLOCKS, send_block, 0)


def unpack_kernel(place, held, out, gram):
    col = place[2]
    low = lane_of((8, LANES)) < 64
    for pair in range(2):
        slabs = [lax.rem(2 * pair + h + col, 4) for h in range(2)]

        def one(r, carry):
            for k in range(4):
                first = held[slabs[0] * 8 + r, k]
                second = held[slabs[1] * 8 + r, k]
                out[pair * 8 + r, k] = jnp.where(low, first, pltpu.roll(second, 64, 1))
                out[pair * 8 + r, k + 4] = jnp.where(low, pltpu.roll(first, 64, 1), second)
            return carry

        lax.fori_loop(0, 8, one, 0)

    size = BANDS * 8

    def dot(a, b, dims):
        return lax.dot_general(
            a, b, (dims, ((), ())), precision=HIGHEST, preferred_element_type=jnp.float32
        )

    products = jnp.zeros((size, size), jnp.float32)
    for x in range(8):
        plane = out[:, x].reshape(size, LANES)
        products += dot(plane, plane, ((1,), (1,)))
    row, lane = row_of((size, size)), lane_of((size, size))
    products = jnp.where((row & 7) == (lane & 7), products, 0.0)
    pick = (row_of((BANDS, size)) == lane_of((BANDS, size)) // 8).astype(jnp.float32)
    rows = dot(pick, products, ((1,), (0,)))
    spread = (row_of((size, LANES)) // 8 == lane_of((size, LANES))).astype(jnp.float32)
    square = dot(rows, spread, ((1,), (0,)))
    gram[...] = square[0:8] + pltpu.roll(square[8:16], BANDS, 1)


def f32(*shape):
    return jax.ShapeDtypeStruct(shape, jnp.float32)


def params(mib=None):
    return pltpu.CompilerParams(vmem_limit_bytes=None if mib is None else mib << 20)


def shards(wave, potential, positions, species, counts, offsets, beta, coupling):
    place = jnp.stack([lax.axis_index("slab"), lax.axis_index("row"), lax.axis_index("col")])
    packed = pl.pallas_call(
        pack_kernel,
        out_shape=f32(BLOCKS, 9, 8, LANES),
        in_specs=[SMEM, SMEM, SMEM, SMEM, VMEM, VMEM],
        out_specs=VMEM,
        compiler_params=params(16),
        name="pack",
    )(place, positions, species, counts, wave, potential)
    held = lax.all_to_all(packed, ("slab", "row"), split_axis=0, concat_axis=0, tiled=True)

    low_edge, high_edge = pl.pallas_call(
        edge_kernel,
        out_shape=(f32(HALO_ROWS, LANES), f32(HALO_ROWS, LANES)),
        in_specs=[VMEM],
        out_specs=(VMEM, VMEM),
        compiler_params=params(16),
        name="edges",
    )(held)

    order = [((h + 2 * pair + col) % 4) * 8 + col for pair in range(2) for col in range(8) for h in range(2)]
    chains = (order[:16], order[16:])
    up = [(a, b) for chain in chains for a, b in zip(chain[:-1], chain[1:])]
    down = [(b, a) for a, b in up]
    low_in = lax.ppermute(high_edge, ("slab", "col"), up)
    high_in = lax.ppermute(low_edge, ("slab", "col"), down)

    sphere = pl.pallas_call(
        sphere_kernel,
        out_shape=f32(beta.shape[0], TILES * 8, LANES),
        in_specs=[VMEM, VMEM],
        out_specs=VMEM,
        name="sphere",
    )(offsets.reshape(-1, offsets.shape[2]), beta)

    filtered = pl.pallas_call(
        filter_kernel,
        out_shape=f32(BLOCKS, 4, 8, LANES),
        in_specs=[SMEM, SMEM, VMEM, VMEM, VMEM, VMEM],
        out_specs=VMEM,
        scratch_shapes=[
            pltpu.VMEM((ROWS, LANES), jnp.float32),
            pltpu.VMEM((ROWS, LANES), jnp.float32),
            pltpu.VMEM((GX * GY, LANES), jnp.float32),
            pltpu.VMEM((GX * GY, LANES), jnp.float32),
            pltpu.VMEM((CAP, TILES * 8, LANES), jnp.float32),
            pltpu.VMEM((CAP, 8, LANES), jnp.float32),
            pltpu.VMEM((CAP, LANES), jnp.float32),
            pltpu.VMEM((2 * BLOCKS, LANES), jnp.int32),
            pltpu.SMEM((2 * BLOCKS, LANES), jnp.int32),
            pltpu.SMEM((CAP + 1,), jnp.int32),
            pltpu.SMEM((2 * CAP + 1,), jnp.int32),
            pltpu.SemaphoreType.DMA,
        ],
        compiler_params=params(56),
        name="filter",
    )(place, coupling, held, low_in, high_in, sphere)

    back = lax.all_to_all(filtered, ("slab", "row"), split_axis=0, concat_axis=0, tiled=True)
    result, partial = pl.pallas_call(
        unpack_kernel,
        out_shape=(f32(*wave.shape), f32(8, LANES)),
        in_specs=[SMEM, VMEM],
        out_specs=(VMEM, VMEM),
        compiler_params=params(16),
        name="unpack",
    )(place, back)

    def total_over(value, axes, count):
        copies = jnp.broadcast_to(value[None], (count,) + value.shape)
        copies = lax.all_to_all(copies, axes, split_axis=0, concat_axis=0, tiled=True)
        return jnp.sum(copies, axis=0)

    partial = total_over(partial, "col", 8)
    partial = total_over(partial, ("slab", "row"), 32)
    gram = jnp.concatenate([partial[:, :BANDS], partial[:, BANDS : 2 * BANDS]], axis=0)
    cells = 4 * 8 * 8 * 8 * 8 * 128
    return result, gram / cells


def solution(mesh):
    in_specs = (
        P(None, "slab", "row", "col"),
        P("slab", "row", "col"),
        P(None, ("slab", "row", "col")),
        P(("slab", "row", "col")),
        P(("slab", "row", "col")),
        P(),
        P(),
        P(),
    )
    out_specs = (P(None, "slab", "row", "col"), P())
    return jax.shard_map(shards, mesh=mesh, in_specs=in_specs, out_specs=out_specs, check_vma=False)
```

time: 1420 us -> 179 us (0.13)
  local copies, waits for them, and re-layouts: 426 us -> 4.71 us
  waiting for transfers between devices: 394 us -> 5.47 us
  starting transfers between devices: 258 us -> 16.7 us
  other arithmetic: 221 us -> 0.73 us
  Pallas kernels: 0 us -> 64.9 us
  blocking collectives: 105 us -> 83.9 us
    ppermute x36 -> x2, waiting for transfers between devices: 394 us -> 5.47 us  [the longest x1 4.39 us: shards(): high_in = lax.ppermute(low_edge, ('slab', 'col'), down)]
    ppermute x36 -> x2, starting transfers between devices: 258 us -> 16.7 us  [the longest x1 14.8 us: shards(): low_in = lax.ppermute(high_edge, ('slab', 'col'), up)]
    scatter-add x15 -> x0, local copies, waits for them, and re-layouts: 164 us -> none  [the longest x6 83.2 us: add_rims(): return inner.at[tuple(trailing)].add(upper_part)]
    psum x1 -> x0, blocking collectives: 105 us -> none  [shards(): summed_gram = lax.psum(partial_gram, ('slab', 'row', 'col'))]
    scatter-add x9 -> x0, other arithmetic: 90.9 us -> none  [the longest x3 81.8 us: spread_rims(): accumulated = jnp.zeros((bands, wide_x * wide_y * wide_z), jnp.float32).a...]
    reshape x9 -> x1, local copies, waits for them, and re-layouts: 88.1 us -> 0.62 us  [shards(): offsets.reshape(-1, offsets.shape[2])]
    all_to_all x0 -> x4, blocking collectives: none -> 83.9 us  [the longest x1 38.8 us: shards(): lax.all_to_all(packed, ('slab', 'row'), split_axis=0, concat_axis=0, tile...]
    slice x54 -> x1, local copies, waits for them, and re-layouts: 79.1 us -> 0.07 us  [shards(): partial[:, :BANDS]]
  transfers between devices with their start and end apart: 36 -> 2, of which waited for: 32 -> 2; matrix products, arithmetic and copies ran while one was open for 7% -> 0% of each run, Pallas kernels for 0% -> 1%
where the time goes in v1:
time: 179 us; the launch traced here: 178 us
  blocking collectives  83.9 us (47%)
  Pallas kernels  64.9 us (36%)
  starting transfers between devices  16.7 us (9%)
  waiting for transfers between devices  5.47 us (3%)
  local copies, waits for them, and re-layouts  4.71 us (3%)
    pallas_call x1, Pallas kernels, shards(): pl.pallas_call(filter_kernel, out_shape=f32(BLOCKS, 4, 8, LANES), in_spec...  54.5 us
    all_to_all x1, blocking collectives, shards(): lax.all_to_all(packed, ('slab', 'row'), split_axis=0, concat_axis=0, tile...  38.8 us
    all_to_all x2, blocking collectives, total_over(): lax.all_to_all(copies, axes, split_axis=0, concat_axis=0, tiled=True)  23.8 us
    all_to_all x1, blocking collectives, shards(): lax.all_to_all(filtered, ('slab', 'row'), split_axis=0, concat_axis=0, ti...  21.3 us
    ppermute x1, starting transfers between devices, shards(): low_in = lax.ppermute(high_edge, ('slab', 'col'), up)  14.8 us
    ppermute x1, waiting for transfers between devices, shards(): high_in = lax.ppermute(low_edge, ('slab', 'col'), down)  4.39 us
    unnamed x21, local copies, waits for them, and re-layouts  4 us
  transfers between devices with their start and end apart: 2, of which 2 were waited for; matrix products, arithmetic and copies ran while one was open for 0% of the time, Pallas kernels for 1%

profile of v1, /device:TPU:1, one launch (start us, length us, event | category | flops | bytes accessed | tf_op | source)
XLA Modules:
  0.0 177.7 jit_solution(9143719133738748197)
XLA Ops:
  1.3 0.1 pad_add_fusion.place
  1.4 0.0 copy-start.1
  1.4 1.0 copy-done.1
  2.4 0.0 copy-start.2
  2.4 0.8 copy-done.2
  3.2 0.0 copy-start.5
  3.2 0.7 copy-done.5
  3.8 0.0 copy-start.6
  3.8 0.7 copy-done.6
  4.5 0.0 copy-start.3
  4.5 1.9 %pack.1 = f32[32,9,8,128]{3,2,1,0:T(8,128)S(1)} custom-call(s32[3]{0:T(128)S(1)} %pad_add_fusion.place, s32[3,8]{1,0:T(4,128)S(1)} %copy-done.5, s32[8]{0:T(128)S(1)} %copy-done.6, s32[1]{0:T(128)S(6)} %copy.13.counts, f32[16,8,8,128]{3,2,1,0:T(8,128)S(1)} %copy-done.1, f32[8,8,128]{2,1,0:T(8,128)S(1)} %copy-done.2), custom_call_target="tpu_custom_call" | custom-call | tf_op jit(solution)/shard_map/pack/pallas_call | solution.py:422
  6.4 38.8 %all_to_all.20.held = f32[32,9,8,128]{3,2,1,0:T(8,128)S(1)} all-to-all(f32[32,9,8,128]{3,2,1,0:T(8,128)S(1)} %pack.1), channel_id=1, replica_groups=mesh['slab'=4,'row'=8,'col'=8] {'slab','row'}, dimensions={0} | all-to-all | bytes 2359296 | tf_op jit(solution)/shard_map/all_to_all | solution.py:430
  45.2 0.0 copy-done.3
  45.2 0.0 copy-start
  45.2 0.0 copy-start.9
  45.2 2.4 %edges.1 = (f32[1056,128]{1,0:T(8,128)S(1)}, f32[1056,128]{1,0:T(8,128)S(1)}) custom-call(f32[32,9,8,128]{3,2,1,0:T(8,128)S(1)} %all_to_all.20.held), custom_call_target="tpu_custom_call" | custom-call | tf_op jit(solution)/shard_map/edges/pallas_call | solution.py:432
  47.6 14.8 %collective-permute-start = (f32[1056,128]{1,0:T(8,128)S(1)}, f32[1056,128]{1,0:T(8,128)S(1)}, u32[]{:S(2)}, u32[]{:S(2)}) collective-permute-start(f32[1056,128]{1,0:T(8,128)S(1)} %get-tuple-element.6), channel_id=1, source_target_pairs={{0,64},{64,65},{65,129},{129,130},{130,194},{194,195},{195,3},{3,4... | collective-permute-start | bytes 1622024 | tf_op jit(solution)/shard_map/ppermute | solution.py:445
  62.4 1.9 %collective-permute-start.1 = (f32[1056,128]{1,0:T(8,128)S(1)}, f32[1056,128]{1,0:T(8,128)S(1)}, u32[]{:S(2)}, u32[]{:S(2)}) collective-permute-start(f32[1056,128]{1,0:T(8,128)S(1)} %get-tuple-element.7), channel_id=1, source_target_pairs={{64,0},{65,64},{129,65},{130,129},{194,130},{195,194},{3,195},{4,3... | collective-permute-start | bytes 1622024 | tf_op jit(solution)/shard_map/ppermute | solution.py:446
  64.3 0.0 copy-done.9
  64.4 0.6 reshape.9.offsets
  65.0 2.6 %sphere.1 = f32[4,96,128]{2,1,0:T(8,128)} custom-call(s32[12,384]{1,0:T(8,128)} %reshape.9.offsets, f32[4,384]{1,0:T(4,128)} %beta.1), custom_call_target="tpu_custom_call" | custom-call | tf_op jit(solution)/shard_map/sphere/pallas_call | solution.py:448
  67.6 0.0 copy-start.4
  67.6 1.1 collective-permute-done.low_in
  68.7 0.0 copy-start.7
  68.7 4.4 %collective-permute-done.1.high_in = f32[1056,128]{1,0:T(8,128)S(1)} collective-permute-done((f32[1056,128]{1,0:T(8,128)S(1)}, f32[1056,128]{1,0:T(8,128)S(1)}, u32[]{:S(2)}, u32[]{:S(2)}) %collective-permute-start.1) | collective-permute-done | bytes 540704 | tf_op jit(solution)/shard_map/ppermute | solution.py:446
  73.1 0.0 copy-done
  73.1 0.0 copy-done.7
  73.1 0.0 copy-start.8
  73.1 0.8 copy-done.8
  73.9 54.5 %filter.1 = f32[32,4,8,128]{3,2,1,0:T(8,128)} custom-call(s32[3]{0:T(128)} %copy-done.3, f32[4]{0:T(128)} %coupling.1, f32[32,9,8,128]{3,2,1,0:T(8,128)} %copy-done, f32[1056,128]{1,0:T(8,128)} %copy-done.7, f32[1056,128]{1,0:T(8,128)} %copy-done.8, f32[4,96,128]{2,1,0:T(8,128)} %sphere.1), custom_call_target="tpu_custom_call" | custom-call | tf_op jit(solution)/shard_map/filter/pallas_call | solution.py:456
  128.4 21.3 %all_to_all.21.held = f32[32,4,8,128]{3,2,1,0:T(8,128)S(1)} all-to-all(f32[32,4,8,128]{3,2,1,0:T(8,128)} %filter.1), channel_id=1, replica_groups=mesh['slab'=4,'row'=8,'col'=8] {'slab','row'}, dimensions={0} | all-to-all | bytes 1048576 | tf_op jit(solution)/shard_map/all_to_all | solution.py:479
  149.7 0.0 copy-done.4
  149.7 3.5 %unpack.1 = (f32[16,8,8,128]{3,2,1,0:T(8,128)}, f32[8,128]{1,0:T(8,128)S(1)}) custom-call(s32[3]{0:T(128)S(1)} %copy-done.4, f32[32,4,8,128]{3,2,1,0:T(8,128)S(1)} %all_to_all.21.held), custom_call_target="tpu_custom_call" | custom-call | tf_op jit(solution)/shard_map/unpack/pallas_call | solution.py:480
  153.2 9.1 %all_to_all.22 = f32[8,8,128]{2,1,0:T(8,128)S(1)} all-to-all(f32[8,8,128]{2,1,0:T(8,128)S(1)} %broadcast_in_dim.4), channel_id=1, replica_groups=mesh['slab'=4,'row'=8,'col'=8] {'col'}, dimensions={0} | all-to-all | bytes 65536 | tf_op jit(solution)/shard_map/all_to_all | solution.py:491
  162.4 14.6 %all_to_all.23 = f32[32,8,128]{2,1,0:T(8,128)S(1)} all-to-all(f32[32,8,128]{2,1,0:T(8,128)S(1)} %broadcast_in_dim.5), channel_id=1, replica_groups=mesh['slab'=4,'row'=8,'col'=8] {'slab','row'}, dimensions={0} | all-to-all | bytes 262144 | tf_op jit(solution)/shard_map/all_to_all | solution.py:491
  177.0 0.1 fusion
  177.1 0.6 maximum_multiply_fusion
  (5 shorter events, 0.1 us)
Async XLA Ops:
  1.4 1.0 copy-start.1
  2.4 0.8 copy-start.2
  3.2 0.7 copy-start.5
  3.8 0.7 copy-start.6
  4.5 40.7 %copy-start.3 = (s32[3]{0:T(128)}, s32[3]{0:T(128)S(1)}, u32[]{:S(2)}) copy-start(s32[3]{0:T(128)S(1)} %pad_add_fusion.place) | copy-start | bytes 40
  45.2 27.9 %copy-start = (f32[32,9,8,128]{3,2,1,0:T(8,128)}, f32[32,9,8,128]{3,2,1,0:T(8,128)S(1)}, u32[]{:S(2)}) copy-start(f32[32,9,8,128]{3,2,1,0:T(8,128)S(1)} %all_to_all.20.held) | copy-start | bytes 3538948
  45.2 19.1 %copy-start.9 = (s32[4,3,384]{2,0,1:T(4,128)S(1)}, s32[4,3,384]{2,0,1:T(4,128)}, u32[]{:S(2)}) copy-start(s32[4,3,384]{2,0,1:T(4,128)} %param.13) | copy-start | bytes 55300
  47.6 21.1 %collective-permute-start = (f32[1056,128]{1,0:T(8,128)S(1)}, f32[1056,128]{1,0:T(8,128)S(1)}, u32[]{:S(2)}, u32[]{:S(2)}) collective-permute-start(f32[1056,128]{1,0:T(8,128)S(1)} %get-tuple-element.6), channel_id=1, source_target_pairs={{0,64},{64,65},{65,129},{129,130},{130,194},{194,195},{195,3},{3,4... | collective-permute-start | bytes 1622024 | tf_op jit(solution)/shard_map/ppermute | solution.py:445
  62.4 10.7 %collective-permute-start.1 = (f32[1056,128]{1,0:T(8,128)S(1)}, f32[1056,128]{1,0:T(8,128)S(1)}, u32[]{:S(2)}, u32[]{:S(2)}) collective-permute-start(f32[1056,128]{1,0:T(8,128)S(1)} %get-tuple-element.7), channel_id=1, source_target_pairs={{64,0},{65,64},{129,65},{130,129},{194,130},{195,194},{3,195},{4,3... | collective-permute-start | bytes 1622024 | tf_op jit(solution)/shard_map/ppermute | solution.py:446
  67.6 82.1 %copy-start.4 = (s32[3]{0:T(128)S(1)}, s32[3]{0:T(128)}, u32[]{:S(2)}) copy-start(s32[3]{0:T(128)} %copy-done.3) | copy-start | bytes 40
  68.7 4.4 %copy-start.7 = (f32[1056,128]{1,0:T(8,128)}, f32[1056,128]{1,0:T(8,128)S(1)}, u32[]{:S(2)}) copy-start(f32[1056,128]{1,0:T(8,128)S(1)} %collective-permute-done.low_in) | copy-start | bytes 1622020
  73.1 0.8 copy-start.8

commit v2 on v1

v2 whole, which is shorter than its diff:
```python
import jax
import jax.numpy as jnp
from jax import lax
from jax.experimental import pallas as pl
from jax.experimental.pallas import tpu as pltpu
from jax.sharding import PartitionSpec as P

stencil_weights = (
    -5369.0 / 1800.0,
    12.0 / 7.0,
    -15.0 / 56.0,
    10.0 / 189.0,
    -1.0 / 112.0,
    2.0 / 1925.0,
    -1.0 / 16632.0,
)
lower_edge = 3.0
upper_edge = 17.0
centre = 0.5 * (upper_edge + lower_edge)
half_width = 0.5 * (upper_edge - lower_edge)

BANDS = 16
GX, GY, LANES = 32, 64, 128
PX, PY = 6, 8
PITCH = GY + 2 * PY
ROWS = (GX + 2 * PX) * PITCH
TILES = 12
BLOCKS = 32
SLOTS = 8
GROUP = 8
UNROLL = 4
CAP = 2 * BLOCKS * SLOTS
HALO_ROWS = BLOCKS * 34
FAR = -4096
VMEM = pl.BlockSpec(memory_space=pltpu.VMEM)
HIGHEST = lax.Precision.HIGHEST


def lane_of(shape):
    return lax.broadcasted_iota(jnp.int32, shape, len(shape) - 1)


def row_of(shape):
    return lax.broadcasted_iota(jnp.int32, shape, len(shape) - 2)


def pack_kernel(
    positions_in,
    species_in,
    counts_in,
    wave_in,
    potential_in,
    out,
    positions,
    species,
    counts,
    wave,
    potential,
    info,
    sems,
):
    copies = [
        pltpu.make_async_copy(potential_in, potential, sems.at[0]),
        pltpu.make_async_copy(positions_in, positions, sems.at[1]),
        pltpu.make_async_copy(species_in, species, sems.at[2]),
        pltpu.make_async_copy(counts_in, counts, sems.at[3]),
        pltpu.make_async_copy(wave_in.at[0:8], wave.at[0:8], sems.at[4]),
        pltpu.make_async_copy(wave_in.at[8:16], wave.at[8:16], sems.at[5]),
    ]
    for copy in copies:
        copy.start()
    for copy in copies[:4]:
        copy.wait()
    col = lax.axis_index("col")
    low = lane_of((8, LANES)) < 64
    live = lane_of((1, SLOTS)) < counts[...]
    spot = (positions[0:1, :] + PX) * PITCH + positions[1:2, :] + PY
    info[...] = jnp.zeros((8, LANES), jnp.float32)
    info[0:1, 0:SLOTS] = jnp.where(live, positions[2:3, :], FAR).astype(jnp.float32)
    info[1:2, 0:SLOTS] = (spot * 4 + species[...]).astype(jnp.float32)

    def halves(tile, other):
        return (
            jnp.where(low, tile, pltpu.roll(other, 64, 1)),
            jnp.where(low, pltpu.roll(tile, 64, 1), other),
        )

    fixed = [halves(potential[k], potential[k + 4]) for k in range(4)]
    for pair in range(2):
        slabs = [lax.rem(2 * pair + h + col, 4) for h in range(2)]
        copies[4 + pair].wait()

        def one(r, carry):
            band = pair * 8 + r
            for k in range(4):
                parts = halves(wave[band, k], wave[band, k + 4])
                for h in range(2):
                    dest = slabs[h] * 8 + r
                    out[dest, k] = parts[h]
                    out[dest, 4 + k] = fixed[k][h]
            for h in range(2):
                out[slabs[h] * 8 + r, 8] = info[...]
            return carry

        lax.fori_loop(0, 8, one, 0)


def edge_kernel(held, low_out, high_out):
    even = (lane_of((8, LANES)) & 32) == 0

    def one(i, carry):
        for d in [i * UNROLL + k for k in range(UNROLL)]:
            for tile in range(4):
                first = held[d, 2 * tile]
                second = pltpu.roll(held[d, 2 * tile + 1], 32, 1)
                at = pl.multiple_of(d * 32, 32) + tile * 8
                low_out[pl.ds(at, 8), :] = jnp.where(even, first, second)
                high_out[pl.ds(at, 8), :] = jnp.where(even, second, first)
        return carry

    lax.fori_loop(0, BLOCKS // UNROLL, one, 0)
    for k in range(2):
        at = BLOCKS * (32 + k)
        rows = held[:, 8, k, :]
        low_out[at : at + BLOCKS, :] = rows
        high_out[at : at + BLOCKS, :] = rows


def sphere_kernel(offsets, beta, coupling, out):
    points = beta.shape[1]
    for kind in range(beta.shape[0]):
        dx = offsets[3 * kind : 3 * kind + 1, :]
        dy = offsets[3 * kind + 1 : 3 * kind + 2, :]
        dz = offsets[3 * kind + 2 : 3 * kind + 3, :]
        row = 16 + (dx + 3) * 8 + dy + 4
        row = jnp.where(jnp.abs(dx) == 4, jnp.where(dx > 0, 8, 0) + dy + 3, row)
        row = jnp.where(dy == 4, 72 + dx + 3, row)
        row = jnp.where(jnp.abs(dy) == 5, jnp.where(dy > 0, 81, 80), row)
        row = jnp.where(jnp.abs(dx) == 5, jnp.where(dx > 0, 89, 88), row)
        left = (row_of((TILES * 8, points)) == row).astype(jnp.float32)
        values = beta[kind : kind + 1, :] * jnp.sqrt(coupling[0:1, kind : kind + 1])
        right = jnp.where(row_of((LANES, points)) == dz + 5, values, 0.0)
        out[kind] = lax.dot_general(
            left,
            right,
            (((1,), (1,)), ((), ())),
            precision=HIGHEST,
            preferred_element_type=jnp.float32,
        )


def tile_refs(ref, base):
    yield ref.at[pl.ds(base - 4 * PITCH - 3, 8), :]
    yield ref.at[pl.ds(base + 4 * PITCH - 3, 8), :]
    for dx in range(-3, 4):
        yield ref.at[pl.ds(base + dx * PITCH - 4, 8), :]
    yield ref.at[pl.ds(base - 3 * PITCH + 4, 8, stride=PITCH), :]
    yield ref.at[pl.ds(base - 5, 2, stride=10), :]
    yield ref.at[pl.ds(base - 5 * PITCH, 2, stride=10 * PITCH), :]


TILE_ROWS = (8,) * 10 + (2, 2)


def filter_kernel(
    held,
    low_in,
    high_in,
    sphere,
    out,
    buf_a,
    buf_b,
    pot,
    rolled,
    acc,
    total,
    table_v,
    table,
    listed,
    sem,
):
    slab, col = lax.axis_index("slab"), lax.axis_index("col")
    half = lax.rem(slab + 4 - lax.rem(col, 4), 4) % 2
    depth = col * 2 + half
    lane8, row8 = lane_of((8, LANES)), row_of((8, LANES))

    both = []
    for k in range(2):
        at = BLOCKS * (32 + k)
        outer = jnp.where(half == 0, low_in[at : at + BLOCKS, :], high_in[at : at + BLOCKS, :])
        both.append(jnp.concatenate([held[:, 8, k, :], outer], axis=0).astype(jnp.int32))
    along, spot = both
    along = along - (depth * 64 - 32)
    code = jnp.where((along >= 7) & (along < 121), 2, 3)
    code = code - jnp.where((along >= 17) & (along < 111), 1, 0)
    code = code - jnp.where((along >= 27) & (along < 101), 1, 0)
    code = jnp.where(spot > 0, code, 3)
    turn = (along - 37) & (LANES - 1)
    table_v[...] = jnp.where(code < 3, spot * 512 + turn * 4 + code, 3)
    copy = pltpu.make_async_copy(table_v, table, sem)
    copy.start()

    edge = PX * PITCH

    def clear_edges(target):
        target[0:edge, :] = jnp.zeros((edge, LANES), jnp.float32)
        target[ROWS - edge :, :] = jnp.zeros((edge, LANES), jnp.float32)

        for x in range(PX, PX + GX):
            at = x * PITCH
            target[at : at + PY, :] = jnp.zeros((PY, LANES), jnp.float32)
            target[at + PY + GY : at + PITCH, :] = jnp.zeros((PY, LANES), jnp.float32)

    clear_edges(buf_a)
    copy.wait()

    low = lane8 < 64
    even = (lane8 & 32) == 0

    def gather_block(d):
        s, r = d // 8, lax.rem(d, 8)
        for field in range(2):
            for pair in range(2):
                at = pl.multiple_of(d * 32, 32) + field * 16 + pair * 8
                above = high_in[pl.ds(at, 8), :]
                below = low_in[pl.ds(at, 8), :]
                evens = jnp.where(even, above, below)
                odds = jnp.where(even, below, above)
                turned = (
                    pltpu.roll(evens, 64, 1),
                    pltpu.roll(odds, 32, 1),
                    evens,
                    pltpu.roll(odds, 96, 1),
                )
                for m in range(2):
                    own = held[d, field * 4 + 2 * pair + m]
                    for high in range(2):
                        x = 4 * high + 2 * pair + m
                        mid = pltpu.roll(own, 64, 1) if high else own
                        tile = jnp.where(low, mid, turned[2 * high + m])
                        if field == 0:
                            to = pl.multiple_of((s * 8 + x + PX) * PITCH + PY + r * 8, 8)
                            buf_a[pl.ds(to, 8), :] = tile
                        else:
                            to = pl.multiple_of((s * 8 + x) * GY + r * 8, 8)
                            pot[pl.ds(to, 8), :] = tile - (centre + stencil_weights[0])

    def blocks(i, lengths):
        for k in range(UNROLL):
            gather_block(i * UNROLL + k)
        words = [
            table[2 * UNROLL * i + k, slot] for k in range(2 * UNROLL) for slot in range(SLOTS)
        ]
        for word in words:
            code = word & 3
            shift = code * 10
            listed[(lax.shift_right_logical(lengths, shift) & 1023) + code * CAP] = word
            lengths = lengths + lax.shift_left(jnp.int32(1), shift)
        return lengths

    lengths = lax.fori_loop(0, BLOCKS // UNROLL, blocks, jnp.int32(0))
    n3, n2, n1 = lengths & 1023, (lengths >> 10) & 1023, (lengths >> 20) & 1023

    def move_second(i, carry):
        listed[n3 + i] = listed[CAP + i]
        return carry

    def move_first(i, carry):
        listed[n3 + n2 + i] = listed[2 * CAP + i]
        return carry

    lax.fori_loop(0, n2, move_second, 0)
    lax.fori_loop(0, n1, move_first, 0)
    for i in range(GROUP - 1):
        listed[n3 + n2 + n1 + i] = (edge + PY) << 11

    apart = jnp.abs(lane_of((LANES, LANES)) - row_of((LANES, LANES)))
    apart = jnp.minimum(apart, LANES - apart)
    band = jnp.zeros((LANES, LANES), jnp.float32)
    for reach in range(7):
        band = jnp.where(apart == reach, -0.5 * stencil_weights[reach], band)
    band_high = band.astype(jnp.bfloat16)
    band_low = (band - band_high.astype(jnp.float32)).astype(jnp.bfloat16)
    band = jnp.concatenate(
        [
            jnp.concatenate([band_high, band_low], axis=1),
            jnp.concatenate([band_high, jnp.zeros_like(band_low)], axis=1),
        ],
        axis=0,
    )

    lanes = lane_of((1, LANES))
    outside = ((lanes >= 96) & (depth == 0)) | ((lanes >= 64) & (lanes < 96) & (depth == 15))
    mask = jnp.where(outside, 0.0, 1.0)

    def local_part(source, target, scale, subtract):
        factor = mask * scale

        def one(r, carry):
            row = pl.multiple_of(r * 8, 8) + PY
            line = [source[pl.ds(row + x * PITCH, 8), :] for x in range(GX + 2 * PX)]
            field = jnp.concatenate(line[PX : PX + GX], axis=0)
            high = field.astype(jnp.bfloat16)
            small = (field - high.astype(jnp.float32)).astype(jnp.bfloat16)
            both = jnp.concatenate([high, small], axis=1)
            part = jnp.dot(both, band, preferred_element_type=jnp.float32)
            part = part[:, :LANES] + part[:, LANES:]
            for x in range(GX):
                at = row + (x + PX) * PITCH
                own = line[x + PX]
                result = part[8 * x : 8 * x + 8] + pot[pl.ds(row - PY + x * GY, 8), :] * own
                for reach in range(1, 7):
                    near = line[x + PX - reach] + line[x + PX + reach]
                    near += source[pl.ds(at - reach, 8), :] + source[pl.ds(at + reach, 8), :]
                    result += (-0.5 * stencil_weights[reach]) * near
                result = result * factor
                if subtract:
                    result -= target[pl.ds(at, 8), :]
                target[pl.ds(at, 8), :] = result
            return carry

        lax.fori_loop(0, GY // 8, one, 0)

    def gather_atoms(source, count, first):
        def one(i, carry):
            sums = []
            for j in [i * GROUP + k for k in range(GROUP)]:
                word = listed[j]
                base = word >> 11
                kind = (word >> 9) & 3
                turn = (word >> 2) & 127
                parts = []
                for t, ref in enumerate(tile_refs(source, base)):
                    rows = slice(8 * t, 8 * t + TILE_ROWS[t])
                    if first:
                        shape = pltpu.roll(sphere[kind, rows, :], turn, 1) * mask
                        rolled[j, rows, :] = shape
                    else:
                        shape = rolled[j, rows, :]
                    parts.append(ref[...] * shape)
                small = parts[10] + parts[11]
                parts[10:] = [jnp.concatenate([small, jnp.zeros((6, LANES), jnp.float32)], axis=0)]
                while len(parts) > 1:
                    rest = parts[len(parts) // 2 * 2 :]
                    parts = [a + b for a, b in zip(parts[::2], parts[1::2])] + rest
                sums.append(parts[0])
            for width in (1, 2, 4):
                keep = (row8 & width) == 0
                sums = [
                    jnp.where(keep, a, b) + pltpu.roll(jnp.where(keep, b, a), width, 0)
                    for a, b in zip(sums[::2], sums[1::2])
                ]
            acc[i] = sums[0]
            return carry

        lax.fori_loop(0, (count + GROUP - 1) // GROUP, one, 0)

    def sum_atoms(count, scale):
        size = 8 * GROUP

        def one(i, carry):
            at = pl.multiple_of(i * size, size)
            part = acc[pl.ds(pl.multiple_of(i * 8, 8), 8)].reshape(size, LANES)
            part = jnp.sum(part, axis=1, keepdims=True) * scale
            total[pl.ds(at, size), :] = jnp.broadcast_to(part, (size, LANES))
            return carry

        lax.fori_loop(0, (count + size - 1) // size, one, 0)

    def spread_atoms(target, count):
        def one(j, carry):
            base = listed[j] >> 11
            q = total[pl.ds(j, 1), :]
            refs = list(tile_refs(target, base))
            values = []
            for t, ref in enumerate(refs):
                size = TILE_ROWS[t]
                values.append(ref[...] + q * rolled[j, 8 * t : 8 * t + size, :])
            for ref, value in zip(refs, values):
                ref[...] = value
            return carry

        lax.fori_loop(0, count, one, 0)

    def step(source, target, scale, subtract, count, first):
        gather_atoms(source, count, first)
        sum_atoms(count, scale)
        local_part(source, target, scale, subtract)
        spread_atoms(target, count)

    step(buf_a, buf_b, 1.0 / half_width, False, n3 + n2 + n1, True)
    clear_edges(buf_b)
    step(buf_b, buf_a, 2.0 / half_width, True, n3 + n2, False)
    clear_edges(buf_a)
    step(buf_a, buf_b, 2.0 / half_width, True, n3, False)

    def send_blocks(i, carry):
        for d in [i * UNROLL + k for k in range(UNROLL)]:
            s, r = d // 8, lax.rem(d, 8)
            for k in range(4):
                at = pl.multiple_of((s * 8 + k + PX) * PITCH + PY + r * 8, 8)
                first = buf_b[pl.ds(at, 8), :]
                second = buf_b[pl.ds(at + 4 * PITCH, 8), :]
                out[d, k] = jnp.where(low, first, pltpu.roll(second, 64, 1))
        return carry

    lax.fori_loop(0, BLOCKS // UNROLL, send_blocks, 0)


def dot(a, b, dims):
    return lax.dot_general(
        a, b, (dims, ((), ())), precision=HIGHEST, preferred_element_type=jnp.float32
    )


def unpack_kernel(held, out, gram):
    col = lax.axis_index("col")
    low = lane_of((8, LANES)) < 64
    for pair in range(2):
        slabs = [lax.rem(2 * pair + h + col, 4) for h in range(2)]

        def one(i, carry):
            for r in [i * UNROLL + k for k in range(UNROLL)]:
                for k in range(4):
                    first = held[slabs[0] * 8 + r, k]
                    second = held[slabs[1] * 8 + r, k]
                    out[pair * 8 + r, k] = jnp.where(low, first, pltpu.roll(second, 64, 1))
                    out[pair * 8 + r, k + 4] = jnp.where(low, pltpu.roll(first, 64, 1), second)
            return carry

        lax.fori_loop(0, 8 // UNROLL, one, 0)

    size = BANDS * 8
    products = jnp.zeros((size, size), jnp.float32)
    for x in range(8):
        plane = out[:, x].reshape(size, LANES)
        products += dot(plane, plane, ((1,), (1,)))
    row, lane = row_of((size, size)), lane_of((size, size))
    products = jnp.where((row & 7) == (lane & 7), products, 0.0)
    pick = (row_of((BANDS, size)) == lane_of((BANDS, size)) // 8).astype(jnp.float32)
    rows = dot(pick, products, ((1,), (0,)))
    spread = (row_of((size, LANES)) // 8 == (lane_of((size, LANES)) & 15)).astype(jnp.float32)
    square = dot(rows, spread, ((1,), (0,)))
    own = (row_of((BANDS, LANES)) & 7) == lane_of((BANDS, LANES)) // BANDS
    square = jnp.where(own, square, 0.0)
    both = [jnp.sum(square[8 * k : 8 * k + 8], axis=0, keepdims=True) for k in range(2)]
    gram[...] = jnp.concatenate(both * (gram.shape[0] // 2), axis=0)


def sum_copies(parts):
    tiles = [parts[8 * i : 8 * i + 8, :] for i in range(parts.shape[0] // 8)]
    while len(tiles) > 1:
        tiles = [a + b for a, b in zip(tiles[::2], tiles[1::2])]
    total = tiles[0] + pltpu.roll(tiles[0], 4, 0)
    return total + pltpu.roll(total, 2, 0)


def middle_kernel(parts, out):
    total = sum_copies(parts)
    for i in range(out.shape[0] // 8):
        out[8 * i : 8 * i + 8, :] = total


def total_kernel(parts, out):
    total = sum_copies(parts)
    rows = jnp.where(row_of((BANDS, LANES)) < 8, total[0:1], total[1:2])
    own = (row_of((BANDS, LANES)) & 7) == lane_of((BANDS, LANES)) // BANDS
    fold = (row_of((LANES, BANDS)) & 15) == lane_of((LANES, BANDS))
    square = dot(jnp.where(own, rows, 0.0), fold.astype(jnp.float32), ((1,), (0,)))
    out[...] = square * (1.0 / (GX * GY * 1024))


def in_hbm(x):
    return pltpu.with_memory_space_constraint(x, pltpu.HBM)


def f32(*shape):
    return jax.ShapeDtypeStruct(shape, jnp.float32)


def params(mib=None):
    return pltpu.CompilerParams(vmem_limit_bytes=None if mib is None else mib << 20)


def filter_call(held, low_in, high_in, sphere):
    return pl.pallas_call(
        filter_kernel,
        out_shape=f32(BLOCKS, 4, 8, LANES),
        in_specs=[VMEM] * 4,
        out_specs=VMEM,
        scratch_shapes=[
            pltpu.VMEM((ROWS, LANES), jnp.float32),
            pltpu.VMEM((ROWS, LANES), jnp.float32),
            pltpu.VMEM((GX * GY, LANES), jnp.float32),
            pltpu.VMEM((CAP + GROUP, TILES * 8, LANES), jnp.float32),
            pltpu.VMEM((CAP // GROUP, 8, LANES), jnp.float32),
            pltpu.VMEM((CAP, LANES), jnp.float32),
            pltpu.VMEM((2 * BLOCKS, LANES), jnp.int32),
            pltpu.SMEM((2 * BLOCKS, LANES), jnp.int32),
            pltpu.SMEM((3 * CAP + 1024,), jnp.int32),
            pltpu.SemaphoreType.DMA,
        ],
        compiler_params=params(40),
        name="filter",
    )(held, low_in, high_in, sphere)


def shards(wave, potential, positions, species, counts, offsets, beta, coupling):
    packed = pl.pallas_call(
        pack_kernel,
        out_shape=f32(BLOCKS, 9, 8, LANES),
        in_specs=[pl.BlockSpec(memory_space=pltpu.HBM)] * 5,
        out_specs=VMEM,
        scratch_shapes=[
            pltpu.VMEM(positions.shape, jnp.int32),
            pltpu.VMEM((1, SLOTS), jnp.int32),
            pltpu.VMEM((1, 1), jnp.int32),
            pltpu.VMEM(wave.shape, jnp.float32),
            pltpu.VMEM(potential.shape, jnp.float32),
            pltpu.VMEM((8, LANES), jnp.float32),
            pltpu.SemaphoreType.DMA((6,)),
        ],
        compiler_params=params(16),
        name="pack",
    )(in_hbm(positions), in_hbm(species[None]), counts[None], in_hbm(wave), in_hbm(potential))
    held = lax.all_to_all(packed, ("slab", "row"), split_axis=0, concat_axis=0, tiled=True)

    low_edge, high_edge = pl.pallas_call(
        edge_kernel,
        out_shape=(f32(HALO_ROWS, LANES), f32(HALO_ROWS, LANES)),
        in_specs=[VMEM],
        out_specs=(VMEM, VMEM),
        compiler_params=params(16),
        name="edges",
    )(held)

    order = [((h + 2 * pair + col) % 4) * 8 + col for pair in range(2) for col in range(8) for h in range(2)]
    chains = (order[:16], order[16:])
    up = [(a, b) for chain in chains for a, b in zip(chain[:-1], chain[1:])]
    down = [(b, a) for a, b in up]
    low_in = lax.ppermute(high_edge, ("slab", "col"), up)
    high_in = lax.ppermute(low_edge, ("slab", "col"), down)

    sphere = pl.pallas_call(
        sphere_kernel,
        out_shape=pltpu.VMEM((beta.shape[0], TILES * 8, LANES), jnp.float32),
        in_specs=[VMEM, VMEM, VMEM],
        out_specs=VMEM,
        name="sphere",
    )(offsets.reshape(-1, offsets.shape[2]), beta, coupling[None])

    filtered = filter_call(held, low_in, high_in, sphere)
    back = lax.all_to_all(filtered, ("slab", "row"), split_axis=0, concat_axis=0, tiled=True)
    result, partial = pl.pallas_call(
        unpack_kernel,
        out_shape=(f32(*wave.shape), f32(512, LANES)),
        in_specs=[VMEM],
        out_specs=(VMEM, VMEM),
        compiler_params=params(16),
        name="unpack",
    )(back)

    parts = lax.all_to_all(
        partial, ("slab", "row", "col"), split_axis=0, concat_axis=0, tiled=True
    )
    gram = pl.pallas_call(
        total_kernel,
        out_shape=f32(BANDS, BANDS),
        in_specs=[VMEM],
        out_specs=VMEM,
        name="total",
    )(parts)
    return result, gram


def solution(mesh):
    in_specs = (
        P(None, "slab", "row", "col"),
        P("slab", "row", "col"),
        P(None, ("slab", "row", "col")),
        P(("slab", "row", "col")),
        P(("slab", "row", "col")),
        P(),
        P(),
        P(),
    )
    out_specs = (P(None, "slab", "row", "col"), P())
    return jax.shard_map(shards, mesh=mesh, in_specs=in_specs, out_specs=out_specs, check_vma=False)
```

time: 179 us -> 142 us (0.79)
  Pallas kernels: 64.9 us -> 31.2 us
  local copies, waits for them, and re-layouts: 4.71 us -> 0.63 us
    pallas_call x3 -> x4, Pallas kernels: 60.6 us -> 27.4 us  [the longest x1 21.6 us: filter_call(): pl.pallas_call(filter_kernel, out_shape=f32(BLOCKS, 4, 8, LANES), in_spec...]
    unnamed x21 -> x3, local copies, waits for them, and re-layouts: 4 us -> 0.01 us
    all_to_all x2 -> x1, blocking collectives: 23.8 us -> 27.3 us  [shards(): lax.all_to_all(partial, ('slab', 'row', 'col'), split_axis=0, concat_axis...]
    all_to_all x1, blocking collectives: 21.3 us -> 19.4 us  [shards(): lax.all_to_all(filtered, ('slab', 'row'), split_axis=0, concat_axis=0, ti...]
where the time goes in v2:
time: 142 us
  blocking collectives  85.5 us (60%)
  Pallas kernels  31.2 us (22%)
  starting transfers between devices  16.7 us (12%)
  waiting for transfers between devices  6.31 us (4%)
    all_to_all x1, blocking collectives, shards(): lax.all_to_all(packed, ('slab', 'row'), split_axis=0, concat_axis=0, tile...  38.8 us
    all_to_all x1, blocking collectives, shards(): lax.all_to_all(partial, ('slab', 'row', 'col'), split_axis=0, concat_axis...  27.3 us
    pallas_call x1, Pallas kernels, filter_call(): pl.pallas_call(filter_kernel, out_shape=f32(BLOCKS, 4, 8, LANES), in_spec...  21.6 us
    all_to_all x1, blocking collectives, shards(): lax.all_to_all(filtered, ('slab', 'row'), split_axis=0, concat_axis=0, ti...  19.4 us
    ppermute x1, starting transfers between devices, shards(): low_in = lax.ppermute(high_edge, ('slab', 'col'), up)  14.8 us
    ppermute x1, waiting for transfers between devices, shards(): high_in = lax.ppermute(low_edge, ('slab', 'col'), down)  4.08 us
  transfers between devices with their start and end apart: 2, of which 2 were waited for; matrix products, arithmetic and copies ran while one was open for 0% of the time, Pallas kernels for 1%

profile of v2, /device:TPU:1, one launch (start us, length us, event | category | flops | bytes accessed | tf_op | source)
XLA Modules:
  0.0 141.7 jit_solution(13371499760534966612)
XLA Ops:
  1.3 2.3 %pack.1 = f32[32,9,8,128]{3,2,1,0:T(8,128)S(1)} custom-call(s32[3,8]{1,0:T(4,128)} %positions_in.1, s32[1,8]{1,0:T(1,128)} %bitcast.8, s32[1,1]{1,0:T(1,128)} %bitcast.5.counts_in, f32[16,8,8,128]{3,2,1,0:T(8,128)} %wave_in.1, f32[8,8,128]{2,1,0:T(8,128)} %potential_in.1), custom_call_target="tpu_custom_call" | custom-call | tf_op jit(solution)/shard_map/pack/pallas_call | solution.py:509
  3.6 38.8 %all_to_all.21.held = f32[32,9,8,128]{3,2,1,0:T(8,128)S(1)} all-to-all(f32[32,9,8,128]{3,2,1,0:T(8,128)S(1)} %pack.1), channel_id=1, replica_groups=mesh['slab'=4,'row'=8,'col'=8] {'slab','row'}, dimensions={0} | all-to-all | bytes 2359296 | tf_op jit(solution)/shard_map/all_to_all | solution.py:526
  42.4 0.0 copy-start
  42.4 1.5 %edges.1 = (f32[1088,128]{1,0:T(8,128)S(1)}, f32[1088,128]{1,0:T(8,128)}) custom-call(f32[32,9,8,128]{3,2,1,0:T(8,128)S(1)} %all_to_all.21.held), custom_call_target="tpu_custom_call" | custom-call | tf_op jit(solution)/shard_map/edges/pallas_call | solution.py:528
  43.9 14.8 %collective-permute-start = (f32[1088,128]{1,0:T(8,128)}, f32[1088,128]{1,0:T(8,128)S(1)}, u32[]{:S(2)}, u32[]{:S(2)}) collective-permute-start(f32[1088,128]{1,0:T(8,128)} %get-tuple-element.6), channel_id=1, source_target_pairs={{0,64},{64,65},{65,129},{129,130},{130,194},{194,195},{195,3},{3,4... | collective-permute-start | bytes 1671176 | tf_op jit(solution)/shard_map/ppermute | solution.py:541
  58.7 1.9 %collective-permute-start.1 = (f32[1088,128]{1,0:T(8,128)S(1)}, f32[1088,128]{1,0:T(8,128)S(1)}, u32[]{:S(2)}, u32[]{:S(2)}) collective-permute-start(f32[1088,128]{1,0:T(8,128)S(1)} %get-tuple-element.7), channel_id=1, source_target_pairs={{64,0},{65,64},{129,65},{130,129},{194,130},{195,194},{3,195},{4,3... | collective-permute-start | bytes 1671176 | tf_op jit(solution)/shard_map/ppermute | solution.py:542
  60.6 0.0 copy-done
  60.6 0.6 reshape.9.offsets
  61.2 2.0 %sphere.1 = f32[4,96,128]{2,1,0:T(8,128)S(1)} custom-call(s32[12,384]{1,0:T(8,128)} %reshape.9.offsets, f32[4,384]{1,0:T(4,128)} %beta.1, f32[1,4]{1,0:T(1,128)} %bitcast.9), custom_call_target="tpu_custom_call" | custom-call | tf_op jit(solution)/shard_map/sphere/pallas_call | solution.py:544
  63.2 2.2 %collective-permute-done.low_in = f32[1088,128]{1,0:T(8,128)S(1)} collective-permute-done((f32[1088,128]{1,0:T(8,128)}, f32[1088,128]{1,0:T(8,128)S(1)}, u32[]{:S(2)}, u32[]{:S(2)}) %collective-permute-start) | collective-permute-done | bytes 557088 | tf_op jit(solution)/shard_map/ppermute | solution.py:541
  65.4 4.1 %collective-permute-done.1.high_in = f32[1088,128]{1,0:T(8,128)S(1)} collective-permute-done((f32[1088,128]{1,0:T(8,128)S(1)}, f32[1088,128]{1,0:T(8,128)S(1)}, u32[]{:S(2)}, u32[]{:S(2)}) %collective-permute-start.1) | collective-permute-done | bytes 557088 | tf_op jit(solution)/shard_map/ppermute | solution.py:542
  69.5 21.6 %filter.1 = f32[32,4,8,128]{3,2,1,0:T(8,128)S(1)} custom-call(f32[32,9,8,128]{3,2,1,0:T(8,128)S(1)} %all_to_all.21.held, f32[1088,128]{1,0:T(8,128)S(1)} %collective-permute-done.low_in, f32[1088,128]{1,0:T(8,128)S(1)} %collective-permute-done.1.high_in, f32[4,96,128]{2,1,0:T(8,128)S(1)} %sphere.1), custom_call_target="tpu_custom_call" | custom-call | tf_op jit(solution)/shard_map/filter/pallas_call | solution.py:486
  91.1 19.4 %all_to_all.22.held = f32[32,4,8,128]{3,2,1,0:T(8,128)S(1)} all-to-all(f32[32,4,8,128]{3,2,1,0:T(8,128)S(1)} %filter.1), channel_id=1, replica_groups=mesh['slab'=4,'row'=8,'col'=8] {'slab','row'}, dimensions={0} | all-to-all | bytes 1048576 | tf_op jit(solution)/shard_map/all_to_all | solution.py:553
  110.5 2.1 %unpack.1 = (f32[16,8,8,128]{3,2,1,0:T(8,128)}, f32[512,128]{1,0:T(8,128)S(1)}) custom-call(f32[32,4,8,128]{3,2,1,0:T(8,128)S(1)} %all_to_all.22.held), custom_call_target="tpu_custom_call" | custom-call | tf_op jit(solution)/shard_map/unpack/pallas_call | solution.py:554
  112.6 27.3 %all_to_all.23 = f32[256,2,128]{2,1,0:T(2,128)} all-to-all(f32[256,2,128]{2,1,0:T(2,128)S(1)} %bitcast.6), channel_id=1, replica_groups=mesh['slab'=4,'row'=8,'col'=8] {'slab','row','col'}, dimensions={0} | all-to-all | bytes 524288 | tf_op jit(solution)/shard_map/all_to_all | solution.py:563
  139.9 1.7 %total.1 = f32[16,16]{1,0:T(8,128)} custom-call(f32[512,128]{1,0:T(8,128)} %bitcast.7), custom_call_target="tpu_custom_call" | custom-call | tf_op jit(solution)/shard_map/total/pallas_call | solution.py:566
  (1 shorter events, 0.0 us)
Async XLA Ops:
  42.4 18.2 %copy-start = (s32[4,3,384]{2,0,1:T(4,128)S(1)}, s32[4,3,384]{2,0,1:T(4,128)}, u32[]{:S(2)}) copy-start(s32[4,3,384]{2,0,1:T(4,128)} %param.13) | copy-start | bytes 55300
  43.9 21.5 %collective-permute-start = (f32[1088,128]{1,0:T(8,128)}, f32[1088,128]{1,0:T(8,128)S(1)}, u32[]{:S(2)}, u32[]{:S(2)}) collective-permute-start(f32[1088,128]{1,0:T(8,128)} %get-tuple-element.6), channel_id=1, source_target_pairs={{0,64},{64,65},{65,129},{129,130},{130,194},{194,195},{195,3},{3,4... | collective-permute-start | bytes 1671176 | tf_op jit(solution)/shard_map/ppermute | solution.py:541
  58.7 10.9 %collective-permute-start.1 = (f32[1088,128]{1,0:T(8,128)S(1)}, f32[1088,128]{1,0:T(8,128)S(1)}, u32[]{:S(2)}, u32[]{:S(2)}) collective-permute-start(f32[1088,128]{1,0:T(8,128)S(1)} %get-tuple-element.7), channel_id=1, source_target_pairs={{64,0},{65,64},{129,65},{130,129},{194,130},{195,194},{3,195},{4,3... | collective-permute-start | bytes 1671176 | tf_op jit(solution)/shard_map/ppermute | solution.py:542

commit v3 on v2

--- a/solution.py
+++ b/solution.py
@@ -24,14 +24,14 @@
 PX, PY = 6, 8
 PITCH = GY + 2 * PY
 ROWS = (GX + 2 * PX) * PITCH
-TILES = 12
+TILES = 11
 BLOCKS = 32
 SLOTS = 8
 GROUP = 8
 UNROLL = 4
-CAP = 2 * BLOCKS * SLOTS
-HALO_ROWS = BLOCKS * 34
-FAR = -4096
+CAP = BLOCKS * SLOTS
+LIST = 1024
+HALO_ROWS = BLOCKS * 33
 VMEM = pl.BlockSpec(memory_space=pltpu.VMEM)
 HIGHEST = lax.Precision.HIGHEST
 
@@ -64,20 +64,23 @@
         pltpu.make_async_copy(positions_in, positions, sems.at[1]),
         pltpu.make_async_copy(species_in, species, sems.at[2]),
         pltpu.make_async_copy(counts_in, counts, sems.at[3]),
-        pltpu.make_async_copy(wave_in.at[0:8], wave.at[0:8], sems.at[4]),
-        pltpu.make_async_copy(wave_in.at[8:16], wave.at[8:16], sems.at[5]),
     ]
+    for piece in range(4):
+        bands = pl.ds(4 * piece, 4)
+        copies.append(
+            pltpu.make_async_copy(wave_in.at[bands], wave.at[bands], sems.at[4 + piece])
+        )
     for copy in copies:
         copy.start()
     for copy in copies[:4]:
         copy.wait()
     col = lax.axis_index("col")
     low = lane_of((8, LANES)) < 64
-    live = lane_of((1, SLOTS)) < counts[...]
-    spot = (positions[0:1, :] + PX) * PITCH + positions[1:2, :] + PY
+    live = jnp.where(lane_of((1, SLOTS)) < counts[...], 1, 0)
+    rows = [positions[k : k + 1, :] for k in range(3)] + [species[...], live]
     info[...] = jnp.zeros((8, LANES), jnp.float32)
-    info[0:1, 0:SLOTS] = jnp.where(live, positions[2:3, :], FAR).astype(jnp.float32)
-    info[1:2, 0:SLOTS] = (spot * 4 + species[...]).astype(jnp.float32)
+    for k, values in enumerate(rows):
+        info[0:1, SLOTS * k : SLOTS * (k + 1)] = values.astype(jnp.float32)
 
     def halves(tile, other):
         return (
@@ -88,9 +91,9 @@
     fixed = [halves(potential[k], potential[k + 4]) for k in range(4)]
     for pair in range(2):
         slabs = [lax.rem(2 * pair + h + col, 4) for h in range(2)]
-        copies[4 + pair].wait()
-
-        def one(r, carry):
+        for r in range(8):
+            if r % 4 == 0:
+                copies[4 + 2 * pair + r // 4].wait()
             band = pair * 8 + r
             for k in range(4):
                 parts = halves(wave[band, k], wave[band, k + 4])
@@ -100,9 +103,6 @@
                     out[dest, 4 + k] = fixed[k][h]
             for h in range(2):
                 out[slabs[h] * 8 + r, 8] = info[...]
-            return carry
-
-        lax.fori_loop(0, 8, one, 0)
 
 
 def edge_kernel(held, low_out, high_out):
@@ -119,14 +119,12 @@
         return carry
 
     lax.fori_loop(0, BLOCKS // UNROLL, one, 0)
-    for k in range(2):
-        at = BLOCKS * (32 + k)
-        rows = held[:, 8, k, :]
-        low_out[at : at + BLOCKS, :] = rows
-        high_out[at : at + BLOCKS, :] = rows
-
-
-def sphere_kernel(offsets, beta, coupling, out):
+    rows = held[:, 8, 0, :]
+    low_out[BLOCKS * 32 :, :] = rows
+    high_out[BLOCKS * 32 :, :] = rows
+
+
+def fill_sphere(offsets, beta, coupling, out):
     points = beta.shape[1]
     for kind in range(beta.shape[0]):
         dx = offsets[3 * kind : 3 * kind + 1, :]
@@ -136,7 +134,7 @@
         row = jnp.where(jnp.abs(dx) == 4, jnp.where(dx > 0, 8, 0) + dy + 3, row)
         row = jnp.where(dy == 4, 72 + dx + 3, row)
         row = jnp.where(jnp.abs(dy) == 5, jnp.where(dy > 0, 81, 80), row)
-        row = jnp.where(jnp.abs(dx) == 5, jnp.where(dx > 0, 89, 88), row)
+        row = jnp.where(jnp.abs(dx) == 5, jnp.where(dx > 0, 83, 82), row)
         left = (row_of((TILES * 8, points)) == row).astype(jnp.float32)
         values = beta[kind : kind + 1, :] * jnp.sqrt(coupling[0:1, kind : kind + 1])
         right = jnp.where(row_of((LANES, points)) == dz + 5, values, 0.0)
@@ -160,6 +158,100 @@
 
 
 TILE_ROWS = (8,) * 10 + (2, 2)
+TILE_AT = tuple(8 * t for t in range(11)) + (82,)
+
+
+def place_along_z():
+    slab, col = lax.axis_index("slab"), lax.axis_index("col")
+    half = lax.rem(slab + 4 - lax.rem(col, 4), 4) % 2
+    return half, col * 2 + half
+
+
+def atom_words(rows, depth):
+    rows = rows.astype(jnp.int32)
+    x, y, along, kind, live = (
+        rows if k == 0 else pltpu.roll(rows, LANES - SLOTS * k, 1) for k in range(5)
+    )
+    along = along - (depth * 64 - 32)
+    code = jnp.where((along >= 7) & (along < 121), 2, 3)
+    code = code - jnp.where((along >= 17) & (along < 111), 1, 0)
+    code = code - jnp.where((along >= 27) & (along < 101), 1, 0)
+    code = jnp.where(live > 0, code, 3)
+    turn = (along - 37) & (LANES - 1)
+    spot = (x + PX) * PITCH + y + PY
+    return jnp.where(code < 3, (spot * 4 + kind) * 512 + turn * 4 + code, 3)
+
+
+def list_rows(table, listed, first_row, count, lengths):
+    words = [table[first_row + k, slot] for k in range(count) for slot in range(SLOTS)]
+    for word in words:
+        code = word & 3
+        shift = code * 10
+        listed[(lax.shift_right_logical(lengths, shift) & 1023) + code * CAP] = word
+        lengths = lengths + lax.shift_left(jnp.int32(1), shift)
+    return lengths
+
+
+def join_lists(listed, lengths):
+    n0, n1, n2 = lengths & 1023, (lengths >> 10) & 1023, (lengths >> 20) & 1023
+
+    def move_second(i, carry):
+        listed[n0 + i] = listed[CAP + i]
+        return carry
+
+    def move_third(i, carry):
+        listed[n0 + n1 + i] = listed[2 * CAP + i]
+        return carry
+
+    lax.fori_loop(0, n1, move_second, 0)
+    lax.fori_loop(0, n2, move_third, 0)
+    for i in range(GROUP - 1):
+        listed[n0 + n1 + n2 + i] = (PX * PITCH + PY) << 11
+    return n0 + n1 + n2, n0 + n1, n0
+
+
+def lane_mask(depth):
+    lanes = lane_of((1, LANES))
+    outside = ((lanes >= 96) & (depth == 0)) | ((lanes >= 64) & (lanes < 96) & (depth == 15))
+    return jnp.where(outside, 0.0, 1.0)
+
+
+def turn_sphere(sphere, word, mask, rolled, j):
+    kind = (word >> 9) & 3
+    turn = (word >> 2) & 127
+    for t in range(TILES):
+        rows = slice(8 * t, 8 * t + 8)
+        rolled[j, rows, :] = pltpu.roll(sphere[kind, rows, :], turn, 1) * mask
+
+
+def atoms_kernel(
+    held, offsets, beta, coupling, sphere, rolled, list_out, table_v, table, listed, sems
+):
+    half, depth = place_along_z()
+    table_v[...] = atom_words(held[:, 8, 0, :], depth)
+    copy = pltpu.make_async_copy(table_v, table, sems.at[0])
+    copy.start()
+    fill_sphere(offsets, beta, coupling, sphere)
+    copy.wait()
+
+    def build(i, lengths):
+        return list_rows(table, listed, 4 * i, 4, lengths)
+
+    lengths = lax.fori_loop(0, BLOCKS // 4, build, jnp.int32(0))
+    counts = join_lists(listed, lengths)
+    for k in range(3):
+        listed[LIST - 3 + k] = counts[k]
+    copy = pltpu.make_async_copy(listed.at[pl.ds(0, LIST)], list_out, sems.at[1])
+    copy.start()
+    mask = lane_mask(depth)
+
+    def turn_group(i, carry):
+        for j in [i * 4 + k for k in range(4)]:
+            turn_sphere(sphere, listed[j], mask, rolled, j)
+        return carry
+
+    lax.fori_loop(0, (counts[0] + 3) // 4, turn_group, 0)
+    copy.wait()
 
 
 def filter_kernel(
@@ -167,38 +259,33 @@
     low_in,
     high_in,
     sphere,
+    rolled,
+    list_in,
     out,
     buf_a,
     buf_b,
     pot,
-    rolled,
+    parts,
+    outer_rolled,
     acc,
     total,
     table_v,
     table,
     listed,
-    sem,
+    outer_listed,
+    sems,
 ):
-    slab, col = lax.axis_index("slab"), lax.axis_index("col")
-    half = lax.rem(slab + 4 - lax.rem(col, 4), 4) % 2
-    depth = col * 2 + half
+    half, depth = place_along_z()
     lane8, row8 = lane_of((8, LANES)), row_of((8, LANES))
 
-    both = []
-    for k in range(2):
-        at = BLOCKS * (32 + k)
-        outer = jnp.where(half == 0, low_in[at : at + BLOCKS, :], high_in[at : at + BLOCKS, :])
-        both.append(jnp.concatenate([held[:, 8, k, :], outer], axis=0).astype(jnp.int32))
-    along, spot = both
-    along = along - (depth * 64 - 32)
-    code = jnp.where((along >= 7) & (along < 121), 2, 3)
-    code = code - jnp.where((along >= 17) & (along < 111), 1, 0)
-    code = code - jnp.where((along >= 27) & (along < 101), 1, 0)
-    code = jnp.where(spot > 0, code, 3)
-    turn = (along - 37) & (LANES - 1)
-    table_v[...] = jnp.where(code < 3, spot * 512 + turn * 4 + code, 3)
-    copy = pltpu.make_async_copy(table_v, table, sem)
-    copy.start()
+    outer = jnp.where(half == 0, low_in[BLOCKS * 32 :, :], high_in[BLOCKS * 32 :, :])
+    table_v[...] = atom_words(outer, depth)
+    copies = [
+        pltpu.make_async_copy(table_v, table, sems.at[0]),
+        pltpu.make_async_copy(list_in, listed, sems.at[1]),
+    ]
+    for copy in copies:
+        copy.start()
 
     edge = PX * PITCH
 
@@ -212,7 +299,8 @@
             target[at + PY + GY : at + PITCH, :] = jnp.zeros((PY, LANES), jnp.float32)
 
     clear_edges(buf_a)
-    copy.wait()
+    for copy in copies:
+        copy.wait()
 
     low = lane8 < 64
     even = (lane8 & 32) == 0
@@ -243,114 +331,101 @@
                             buf_a[pl.ds(to, 8), :] = tile
                         else:
                             to = pl.multiple_of((s * 8 + x) * GY + r * 8, 8)
-                            pot[pl.ds(to, 8), :] = tile - (centre + stencil_weights[0])
+                            pot[pl.ds(to, 8), :] = tile - (centre + 1.5 * stencil_weights[0])
 
     def blocks(i, lengths):
         for k in range(UNROLL):
             gather_block(i * UNROLL + k)
-        words = [
-            table[2 * UNROLL * i + k, slot] for k in range(2 * UNROLL) for slot in range(SLOTS)
-        ]
-        for word in words:
-            code = word & 3
-            shift = code * 10
-            listed[(lax.shift_right_logical(lengths, shift) & 1023) + code * CAP] = word
-            lengths = lengths + lax.shift_left(jnp.int32(1), shift)
-        return lengths
+        return list_rows(table, outer_listed, UNROLL * i, UNROLL, lengths)
 
     lengths = lax.fori_loop(0, BLOCKS // UNROLL, blocks, jnp.int32(0))
-    n3, n2, n1 = lengths & 1023, (lengths >> 10) & 1023, (lengths >> 20) & 1023
-
-    def move_second(i, carry):
-        listed[n3 + i] = listed[CAP + i]
-        return carry
-
-    def move_first(i, carry):
-        listed[n3 + n2 + i] = listed[2 * CAP + i]
-        return carry
-
-    lax.fori_loop(0, n2, move_second, 0)
-    lax.fori_loop(0, n1, move_first, 0)
-    for i in range(GROUP - 1):
-        listed[n3 + n2 + n1 + i] = (edge + PY) << 11
+    outer_counts = join_lists(outer_listed, lengths)
+    own_counts = [listed[LIST - 3 + k] for k in range(3)]
+    own_groups = (own_counts[0] + GROUP - 1) // GROUP
 
     apart = jnp.abs(lane_of((LANES, LANES)) - row_of((LANES, LANES)))
     apart = jnp.minimum(apart, LANES - apart)
     band = jnp.zeros((LANES, LANES), jnp.float32)
-    for reach in range(7):
+    for reach in range(1, 7):
         band = jnp.where(apart == reach, -0.5 * stencil_weights[reach], band)
-    band_high = band.astype(jnp.bfloat16)
-    band_low = (band - band_high.astype(jnp.float32)).astype(jnp.bfloat16)
-    band = jnp.concatenate(
+    z_high = band.astype(jnp.bfloat16)
+    z_low = (band - z_high.astype(jnp.float32)).astype(jnp.bfloat16)
+    z_band = jnp.concatenate(
         [
-            jnp.concatenate([band_high, band_low], axis=1),
-            jnp.concatenate([band_high, jnp.zeros_like(band_low)], axis=1),
+            jnp.concatenate([z_high, z_low], axis=1),
+            jnp.concatenate([z_high, jnp.zeros_like(z_low)], axis=1),
         ],
         axis=0,
     )
-
-    lanes = lane_of((1, LANES))
-    outside = ((lanes >= 96) & (depth == 0)) | ((lanes >= 64) & (lanes < 96) & (depth == 15))
-    mask = jnp.where(outside, 0.0, 1.0)
+    planes = 4
+    mask = lane_mask(depth)
+
+    def products(source, g, slot):
+        first = g * (planes * PITCH) + PX * PITCH + PY
+        field = jnp.concatenate(
+            [source[pl.ds(first + x * PITCH, GY), :] for x in range(planes)], axis=0
+        )
+        high = field.astype(jnp.bfloat16)
+        small = (field - high.astype(jnp.float32)).astype(jnp.bfloat16)
+        both = jnp.concatenate([high, small], axis=1)
+        along_z = jnp.dot(both, z_band, preferred_element_type=jnp.float32)
+        parts[slot] = along_z[:, :LANES] + along_z[:, LANES:]
 
     def local_part(source, target, scale, subtract):
         factor = mask * scale
 
-        def one(r, carry):
-            row = pl.multiple_of(r * 8, 8) + PY
-            line = [source[pl.ds(row + x * PITCH, 8), :] for x in range(GX + 2 * PX)]
-            field = jnp.concatenate(line[PX : PX + GX], axis=0)
-            high = field.astype(jnp.bfloat16)
-            small = (field - high.astype(jnp.float32)).astype(jnp.bfloat16)
-            both = jnp.concatenate([high, small], axis=1)
-            part = jnp.dot(both, band, preferred_element_type=jnp.float32)
-            part = part[:, :LANES] + part[:, LANES:]
-            for x in range(GX):
-                at = row + (x + PX) * PITCH
-                own = line[x + PX]
-                result = part[8 * x : 8 * x + 8] + pot[pl.ds(row - PY + x * GY, 8), :] * own
-                for reach in range(1, 7):
-                    near = line[x + PX - reach] + line[x + PX + reach]
-                    near += source[pl.ds(at - reach, 8), :] + source[pl.ds(at + reach, 8), :]
-                    result += (-0.5 * stencil_weights[reach]) * near
-                result = result * factor
-                if subtract:
-                    result -= target[pl.ds(at, 8), :]
-                target[pl.ds(at, 8), :] = result
+        def one(g, carry, more=True):
+            slot = g & 1
+            first = g * (planes * PITCH) + PX * PITCH + PY
+            for t in range(GY // 8):
+                line = [
+                    source[pl.ds(first + (x - PX) * PITCH + 8 * t, 8), :]
+                    for x in range(planes + 2 * PX)
+                ]
+                for x in range(planes):
+                    at = x * GY + 8 * t
+                    own_at = g * (planes * GY) + at
+                    to = first + x * PITCH + 8 * t
+                    result = parts[slot, at : at + 8, :] + pot[pl.ds(own_at, 8), :] * line[x + PX]
+                    for reach in range(1, 7):
+                        near = line[x + PX - reach] + line[x + PX + reach]
+                        near += source[pl.ds(to - reach, 8), :] + source[pl.ds(to + reach, 8), :]
+                        result += (-0.5 * stencil_weights[reach]) * near
+                    result = result * factor
+                    if subtract:
+                        result -= target[pl.ds(to, 8), :]
+                    target[pl.ds(to, 8), :] = result
+            if more:
+                products(source, g + 1, 1 - slot)
             return carry
 
-        lax.fori_loop(0, GY // 8, one, 0)
-
-    def gather_atoms(source, count, first):
+        products(source, 0, 0)
+        for g in range(GX // planes):
+            one(g, 0, g < GX // planes - 1)
+
+    def gather_atoms(source, atoms, tables, count, first_group, turn):
         def one(i, carry):
             sums = []
             for j in [i * GROUP + k for k in range(GROUP)]:
-                word = listed[j]
-                base = word >> 11
-                kind = (word >> 9) & 3
-                turn = (word >> 2) & 127
-                parts = []
-                for t, ref in enumerate(tile_refs(source, base)):
-                    rows = slice(8 * t, 8 * t + TILE_ROWS[t])
-                    if first:
-                        shape = pltpu.roll(sphere[kind, rows, :], turn, 1) * mask
-                        rolled[j, rows, :] = shape
-                    else:
-                        shape = rolled[j, rows, :]
-                    parts.append(ref[...] * shape)
-                small = parts[10] + parts[11]
-                parts[10:] = [jnp.concatenate([small, jnp.zeros((6, LANES), jnp.float32)], axis=0)]
-                while len(parts) > 1:
-                    rest = parts[len(parts) // 2 * 2 :]
-                    parts = [a + b for a, b in zip(parts[::2], parts[1::2])] + rest
-                sums.append(parts[0])
+                word = atoms[j]
+                if turn:
+                    turn_sphere(sphere, word, mask, tables, j)
+                terms = []
+                for t, ref in enumerate(tile_refs(source, word >> 11)):
+                    terms.append(ref[...] * tables[j, TILE_AT[t] : TILE_AT[t] + TILE_ROWS[t], :])
+                small = terms[10] + terms[11]
+                terms[10:] = [jnp.concatenate([small, jnp.zeros((6, LANES), jnp.float32)], axis=0)]
+                while len(terms) > 1:
+                    rest = terms[len(terms) // 2 * 2 :]
+                    terms = [a + b for a, b in zip(terms[::2], terms[1::2])] + rest
+                sums.append(terms[0])
             for width in (1, 2, 4):
                 keep = (row8 & width) == 0
                 sums = [
                     jnp.where(keep, a, b) + pltpu.roll(jnp.where(keep, b, a), width, 0)
                     for a, b in zip(sums[::2], sums[1::2])
                 ]
-            acc[i] = sums[0]
+            acc[first_group + i] = sums[0]
             return carry
 
         lax.fori_loop(0, (count + GROUP - 1) // GROUP, one, 0)
@@ -367,32 +442,33 @@
 
         lax.fori_loop(0, (count + size - 1) // size, one, 0)
 
-    def spread_atoms(target, count):
+    def spread_atoms(target, atoms, tables, count, first):
         def one(j, carry):
-            base = listed[j] >> 11
-            q = total[pl.ds(j, 1), :]
-            refs = list(tile_refs(target, base))
+            q = total[pl.ds(first + j, 1), :]
+            refs = list(tile_refs(target, atoms[j] >> 11))
             values = []
             for t, ref in enumerate(refs):
-                size = TILE_ROWS[t]
-                values.append(ref[...] + q * rolled[j, 8 * t : 8 * t + size, :])
+                values.append(ref[...] + q * tables[j, TILE_AT[t] : TILE_AT[t] + TILE_ROWS[t], :])
             for ref, value in zip(refs, values):
                 ref[...] = value
             return carry
 
         lax.fori_loop(0, count, one, 0)
 
-    def step(source, target, scale, subtract, count, first):
-        gather_atoms(source, count, first)
-        sum_atoms(count, scale)
+    def step(source, target, scale, subtract, which):
+        own, outer = own_counts[which], outer_counts[which]
+        gather_atoms(source, listed, rolled, own, 0, False)
+        gather_atoms(source, outer_listed, outer_rolled, outer, own_groups, which == 0)
+        sum_atoms(own_groups * GROUP + outer, scale)
         local_part(source, target, scale, subtract)
-        spread_atoms(target, count)
-
-    step(buf_a, buf_b, 1.0 / half_width, False, n3 + n2 + n1, True)
+        spread_atoms(target, listed, rolled, own, 0)
+        spread_atoms(target, outer_listed, outer_rolled, outer, own_groups * GROUP)
+
+    step(buf_a, buf_b, 1.0 / half_width, False, 0)
     clear_edges(buf_b)
-    step(buf_b, buf_a, 2.0 / half_width, True, n3 + n2, False)
+    step(buf_b, buf_a, 2.0 / half_width, True, 1)
     clear_edges(buf_a)
-    step(buf_a, buf_b, 2.0 / half_width, True, n3, False)
+    step(buf_a, buf_b, 2.0 / half_width, True, 2)
 
     def send_blocks(i, carry):
         for d in [i * UNROLL + k for k in range(UNROLL)]:
@@ -482,27 +558,54 @@
     return pltpu.CompilerParams(vmem_limit_bytes=None if mib is None else mib << 20)
 
 
-def filter_call(held, low_in, high_in, sphere):
+ATOM_TABLES = (CAP + GROUP, TILES * 8, LANES)
+
+
+def atoms_call(held, offsets, beta, coupling):
+    return pl.pallas_call(
+        atoms_kernel,
+        out_shape=(
+            pltpu.VMEM((beta.shape[0], TILES * 8, LANES), jnp.float32),
+            pltpu.VMEM(ATOM_TABLES, jnp.float32),
+            pltpu.VMEM((LIST,), jnp.int32),
+        ),
+        in_specs=[VMEM] * 4,
+        out_specs=(VMEM,) * 3,
+        scratch_shapes=[
+            pltpu.VMEM((BLOCKS, LANES), jnp.int32),
+            pltpu.SMEM((BLOCKS, LANES), jnp.int32),
+            pltpu.SMEM((3 * CAP + 1024,), jnp.int32),
+            pltpu.SemaphoreType.DMA((2,)),
+        ],
+        compiler_params=params(20),
+        cost_estimate=pl.CostEstimate(flops=10**8, bytes_accessed=10**7, transcendentals=0),
+        name="atoms",
+    )(held, offsets, beta, coupling)
+
+
+def filter_call(held, low_in, high_in, sphere, rolled, atom_list):
     return pl.pallas_call(
         filter_kernel,
         out_shape=f32(BLOCKS, 4, 8, LANES),
-        in_specs=[VMEM] * 4,
+        in_specs=[VMEM] * 6,
         out_specs=VMEM,
         scratch_shapes=[
             pltpu.VMEM((ROWS, LANES), jnp.float32),
             pltpu.VMEM((ROWS, LANES), jnp.float32),
             pltpu.VMEM((GX * GY, LANES), jnp.float32),
-            pltpu.VMEM((CAP + GROUP, TILES * 8, LANES), jnp.float32),
-            pltpu.VMEM((CAP // GROUP, 8, LANES), jnp.float32),
-            pltpu.VMEM((CAP, LANES), jnp.float32),
-            pltpu.VMEM((2 * BLOCKS, LANES), jnp.int32),
-            pltpu.SMEM((2 * BLOCKS, LANES), jnp.int32),
+            pltpu.VMEM((2, 4 * GY, LANES), jnp.float32),
+            pltpu.VMEM(ATOM_TABLES, jnp.float32),
+            pltpu.VMEM((2 * CAP // GROUP, 8, LANES), jnp.float32),
+            pltpu.VMEM((2 * CAP, LANES), jnp.float32),
+            pltpu.VMEM((BLOCKS, LANES), jnp.int32),
+            pltpu.SMEM((BLOCKS, LANES), jnp.int32),
+            pltpu.SMEM((LIST,), jnp.int32),
             pltpu.SMEM((3 * CAP + 1024,), jnp.int32),
-            pltpu.SemaphoreType.DMA,
+            pltpu.SemaphoreType.DMA((2,)),
         ],
-        compiler_params=params(40),
+        compiler_params=params(28),
         name="filter",
-    )(held, low_in, high_in, sphere)
+    )(held, low_in, high_in, sphere, rolled, atom_list)
 
 
 def shards(wave, potential, positions, species, counts, offsets, beta, coupling):
@@ -518,7 +621,7 @@
             pltpu.VMEM(wave.shape, jnp.float32),
             pltpu.VMEM(potential.shape, jnp.float32),
             pltpu.VMEM((8, LANES), jnp.float32),
-            pltpu.SemaphoreType.DMA((6,)),
+            pltpu.SemaphoreType.DMA((8,)),
         ],
         compiler_params=params(16),
         name="pack",
@@ -541,15 +644,8 @@
     low_in = lax.ppermute(high_edge, ("slab", "col"), up)
     high_in = lax.ppermute(low_edge, ("slab", "col"), down)
 
-    sphere = pl.pallas_call(
-        sphere_kernel,
-        out_shape=pltpu.VMEM((beta.shape[0], TILES * 8, LANES), jnp.float32),
-        in_specs=[VMEM, VMEM, VMEM],
-        out_specs=VMEM,
-        name="sphere",
-    )(offsets.reshape(-1, offsets.shape[2]), beta, coupling[None])
-
-    filtered = filter_call(held, low_in, high_in, sphere)
+    atoms = atoms_call(held, offsets.reshape(-1, offsets.shape[2]), beta, coupling[None])
+    filtered = filter_call(held, low_in, high_in, *atoms)
     back = lax.all_to_all(filtered, ("slab", "row"), split_axis=0, concat_axis=0, tiled=True)
     result, partial = pl.pallas_call(
         unpack_kernel,

time: 142 us -> 136 us (0.958)
  waiting for transfers between devices: 6.31 us -> 1.89 us
  blocking collectives: 85.5 us -> 83.1 us
    pallas_call x1, Pallas kernels: 1.96 us -> 6.78 us  [atoms_call(): pl.pallas_call(atoms_kernel, out_shape=(pltpu.VMEM((beta.shape[0], TILES...]
    all_to_all x1, blocking collectives: 19.4 us -> 16.9 us  [shards(): lax.all_to_all(filtered, ('slab', 'row'), split_axis=0, concat_axis=0, ti...]
    ppermute x1, waiting for transfers between devices: 2.23 us -> 0.01 us  [shards(): low_in = lax.ppermute(high_edge, ('slab', 'col'), up)]
    ppermute x1, waiting for transfers between devices: 4.08 us -> 1.88 us  [shards(): high_in = lax.ppermute(low_edge, ('slab', 'col'), down)]
    pallas_call x1, Pallas kernels: 21.6 us -> 19.8 us  [filter_call(): pl.pallas_call(filter_kernel, out_shape=f32(BLOCKS, 4, 8, LANES), in_spec...]
  transfers between devices with their start and end apart: 2 -> 2, of which waited for: 2 -> 1; matrix products, arithmetic and copies ran while one was open for 0% -> 0% of each run, Pallas kernels for 1% -> 5%
where the time goes in v3:
time: 136 us
  blocking collectives  83.1 us (61%)
  Pallas kernels  32.6 us (24%)
  starting transfers between devices  16.7 us (12%)
  waiting for transfers between devices  1.89 us (1%)
  between operations  1.38 us (1%)
    all_to_all x1, blocking collectives, shards(): lax.all_to_all(packed, ('slab', 'row'), split_axis=0, concat_axis=0, tile...  38.8 us
    all_to_all x1, blocking collectives, shards(): lax.all_to_all(partial, ('slab', 'row', 'col'), split_axis=0, concat_axis...  27.4 us
    pallas_call x1, Pallas kernels, filter_call(): pl.pallas_call(filter_kernel, out_shape=f32(BLOCKS, 4, 8, LANES), in_spec...  19.8 us
    all_to_all x1, blocking collectives, shards(): lax.all_to_all(filtered, ('slab', 'row'), split_axis=0, concat_axis=0, ti...  16.9 us
    ppermute x1, starting transfers between devices, shards(): low_in = lax.ppermute(high_edge, ('slab', 'col'), up)  14.8 us
    pallas_call x1, Pallas kernels, atoms_call(): pl.pallas_call(atoms_kernel, out_shape=(pltpu.VMEM((beta.shape[0], TILES...  6.78 us
  transfers between devices with their start and end apart: 2, of which 1 were waited for; matrix products, arithmetic and copies ran while one was open for 0% of the time, Pallas kernels for 5%

profile of v3, /device:TPU:1, one launch (start us, length us, event | category | flops | bytes accessed | tf_op | source)
XLA Modules:
  0.0 135.6 jit_solution(2888538066587318516)
XLA Ops:
  1.3 1.4 %pack.1 = f32[32,9,8,128]{3,2,1,0:T(8,128)S(1)} custom-call(s32[3,8]{1,0:T(4,128)} %positions_in.1, s32[1,8]{1,0:T(1,128)} %bitcast.9, s32[1,1]{1,0:T(1,128)} %bitcast.5.counts_in, f32[16,8,8,128]{3,2,1,0:T(8,128)} %wave_in.1, f32[8,8,128]{2,1,0:T(8,128)} %potential_in.1), custom_call_target="tpu_custom_call" | custom-call | tf_op jit(solution)/shard_map/pack/pallas_call | solution.py:612
  2.7 38.8 %all_to_all.21.held = f32[32,9,8,128]{3,2,1,0:T(8,128)S(1)} all-to-all(f32[32,9,8,128]{3,2,1,0:T(8,128)S(1)} %pack.1), channel_id=1, replica_groups=mesh['slab'=4,'row'=8,'col'=8] {'slab','row'}, dimensions={0} | all-to-all | bytes 2359296 | tf_op jit(solution)/shard_map/all_to_all | solution.py:629
  41.5 0.0 copy-start.2
  41.5 0.0 copy-start
  41.5 0.0 copy-start.1
  41.5 0.7 edges.1
  42.2 14.8 %collective-permute-start = (f32[1056,128]{1,0:T(8,128)S(1)}, f32[1056,128]{1,0:T(8,128)S(1)}, u32[]{:S(2)}, u32[]{:S(2)}) collective-permute-start(f32[1056,128]{1,0:T(8,128)S(1)} %get-tuple-element.9), channel_id=1, source_target_pairs={{0,64},{64,65},{65,129},{129,130},{130,194},{194,195},{195,3},{3,4... | collective-permute-start | bytes 1622024 | tf_op jit(solution)/shard_map/ppermute | solution.py:644
  57.0 1.9 %collective-permute-start.1 = (f32[1056,128]{1,0:T(8,128)S(1)}, f32[1056,128]{1,0:T(8,128)S(1)}, u32[]{:S(2)}, u32[]{:S(2)}) collective-permute-start(f32[1056,128]{1,0:T(8,128)S(1)} %get-tuple-element.10), channel_id=1, source_target_pairs={{64,0},{65,64},{129,65},{130,129},{194,130},{195,194},{3,195},{4,3... | collective-permute-start | bytes 1622024 | tf_op jit(solution)/shard_map/ppermute | solution.py:645
  58.9 0.0 copy-done.2
  59.0 0.0 copy-done
  59.0 0.0 copy-done.1
  59.0 6.8 %atoms.1 = (f32[4,88,128]{2,1,0:T(8,128)S(1)}, f32[264,88,128]{2,1,0:T(8,128)S(1)}, s32[1024]{0:T(1024)S(1)}) custom-call(f32[32,9,8,128]{3,2,1,0:T(8,128)S(1)} %all_to_all.21.held, s32[12,384]{1,0:T(8,128)S(1)} %reshape.9.offsets, f32[4,384]{1,0:T(4,128)S(1)} %copy-done, f32[1,4]{1,0:T(1,128)S(1)} %bitcast.7), custom_call_target="tpu_custom_call" | custom-call | flops 100000000 | bytes 10000000 | tf_op jit(solution)/shard_map/atoms/pallas_call | solution.py:565
  65.8 0.0 collective-permute-done.low_in
  65.8 1.9 %collective-permute-done.1.high_in = f32[1056,128]{1,0:T(8,128)S(1)} collective-permute-done((f32[1056,128]{1,0:T(8,128)S(1)}, f32[1056,128]{1,0:T(8,128)S(1)}, u32[]{:S(2)}, u32[]{:S(2)}) %collective-permute-start.1) | collective-permute-done | bytes 540704 | tf_op jit(solution)/shard_map/ppermute | solution.py:645
  67.7 19.8 %filter.1 = f32[32,4,8,128]{3,2,1,0:T(8,128)S(1)} custom-call(f32[32,9,8,128]{3,2,1,0:T(8,128)S(1)} %all_to_all.21.held, f32[1056,128]{1,0:T(8,128)S(1)} %collective-permute-done.low_in, f32[1056,128]{1,0:T(8,128)S(1)} %collective-permute-done.1.high_in, f32[4,88,128]{2,1,0:T(8,128)S(1)} %get-tuple-element.11.sphere, ...), custom_call_target="tpu_custom_call" | custom-call | tf_op jit(solution)/shard_map/filter/pallas_call | solution.py:587
  87.5 16.9 %all_to_all.22.held = f32[32,4,8,128]{3,2,1,0:T(8,128)S(1)} all-to-all(f32[32,4,8,128]{3,2,1,0:T(8,128)S(1)} %filter.1), channel_id=1, replica_groups=mesh['slab'=4,'row'=8,'col'=8] {'slab','row'}, dimensions={0} | all-to-all | bytes 1048576 | tf_op jit(solution)/shard_map/all_to_all | solution.py:649
  104.4 2.1 %unpack.1 = (f32[16,8,8,128]{3,2,1,0:T(8,128)}, f32[512,128]{1,0:T(8,128)S(1)}) custom-call(f32[32,4,8,128]{3,2,1,0:T(8,128)S(1)} %all_to_all.22.held), custom_call_target="tpu_custom_call" | custom-call | tf_op jit(solution)/shard_map/unpack/pallas_call | solution.py:650
  106.5 27.4 %all_to_all.23 = f32[256,2,128]{2,1,0:T(2,128)} all-to-all(f32[256,2,128]{2,1,0:T(2,128)S(1)} %bitcast.6), channel_id=1, replica_groups=mesh['slab'=4,'row'=8,'col'=8] {'slab','row','col'}, dimensions={0} | all-to-all | bytes 524288 | tf_op jit(solution)/shard_map/all_to_all | solution.py:659
  133.9 1.7 %total.1 = f32[16,16]{1,0:T(8,128)} custom-call(f32[512,128]{1,0:T(8,128)} %bitcast.8), custom_call_target="tpu_custom_call" | custom-call | tf_op jit(solution)/shard_map/total/pallas_call | solution.py:662
  (2 shorter events, 0.0 us)
Async XLA Ops:
  41.5 17.4 %copy-start.2 = (s32[4,3,384]{2,0,1:T(4,128)S(1)}, s32[4,3,384]{2,0,1:T(4,128)}, u32[]{:S(2)}) copy-start(s32[4,3,384]{2,0,1:T(4,128)} %param.13) | copy-start | bytes 55300
  41.5 17.5 %copy-start = (f32[4,384]{1,0:T(4,128)S(1)}, f32[4,384]{1,0:T(4,128)}, u32[]{:S(2)}) copy-start(f32[4,384]{1,0:T(4,128)} %beta.1) | copy-start | bytes 18436
  41.5 17.5 %copy-start.1 = (f32[4]{0:T(128)S(1)}, f32[4]{0:T(128)}, u32[]{:S(2)}) copy-start(f32[4]{0:T(128)} %param.15) | copy-start | bytes 52
  42.2 23.6 %collective-permute-start = (f32[1056,128]{1,0:T(8,128)S(1)}, f32[1056,128]{1,0:T(8,128)S(1)}, u32[]{:S(2)}, u32[]{:S(2)}) collective-permute-start(f32[1056,128]{1,0:T(8,128)S(1)} %get-tuple-element.9), channel_id=1, source_target_pairs={{0,64},{64,65},{65,129},{129,130},{130,194},{194,195},{195,3},{3,4... | collective-permute-start | bytes 1622024 | tf_op jit(solution)/shard_map/ppermute | solution.py:644
  57.0 10.7 %collective-permute-start.1 = (f32[1056,128]{1,0:T(8,128)S(1)}, f32[1056,128]{1,0:T(8,128)S(1)}, u32[]{:S(2)}, u32[]{:S(2)}) collective-permute-start(f32[1056,128]{1,0:T(8,128)S(1)} %get-tuple-element.10), channel_id=1, source_target_pairs={{64,0},{65,64},{129,65},{130,129},{194,130},{195,194},{3,195},{4,3... | collective-permute-start | bytes 1622024 | tf_op jit(solution)/shard_map/ppermute | solution.py:645

commit v4 on v3

--- a/solution.py
+++ b/solution.py
@@ -26,6 +26,7 @@
 ROWS = (GX + 2 * PX) * PITCH
 TILES = 11
 BLOCKS = 32
+DEVICES = 256
 SLOTS = 8
 GROUP = 8
 UNROLL = 4
@@ -510,17 +511,31 @@
     products = jnp.zeros((size, size), jnp.float32)
     for x in range(8):
         plane = out[:, x].reshape(size, LANES)
-        products += dot(plane, plane, ((1,), (1,)))
+        high = plane.astype(jnp.bfloat16)
+        small = (plane - high.astype(jnp.float32)).astype(jnp.bfloat16)
+        products += lax.dot_general(
+            jnp.concatenate([high, high, small], axis=1),
+            jnp.concatenate([high, small, high], axis=1),
+            (((1,), (1,)), ((), ())),
+            preferred_element_type=jnp.float32,
+        )
     row, lane = row_of((size, size)), lane_of((size, size))
     products = jnp.where((row & 7) == (lane & 7), products, 0.0)
-    pick = (row_of((BANDS, size)) == lane_of((BANDS, size)) // 8).astype(jnp.float32)
-    rows = dot(pick, products, ((1,), (0,)))
-    spread = (row_of((size, LANES)) // 8 == (lane_of((size, LANES)) & 15)).astype(jnp.float32)
-    square = dot(rows, spread, ((1,), (0,)))
-    own = (row_of((BANDS, LANES)) & 7) == lane_of((BANDS, LANES)) // BANDS
-    square = jnp.where(own, square, 0.0)
-    both = [jnp.sum(square[8 * k : 8 * k + 8], axis=0, keepdims=True) for k in range(2)]
-    gram[...] = jnp.concatenate(both * (gram.shape[0] // 2), axis=0)
+    rows = jnp.sum(products.reshape(BANDS, 8, LANES), axis=1)
+    for width in (1, 2, 4):
+        rows = rows + pltpu.roll(rows, LANES - width, 1)
+    rows = jnp.where((lane_of((BANDS, LANES)) & 7) == 0, rows, 0.0)
+    both = [
+        jnp.sum(
+            pltpu.roll(rows[8 * k : 8 * k + 8], 0, 1, stride=1, stride_axis=0),
+            axis=0,
+            keepdims=True,
+        )
+        for k in range(2)
+    ]
+    tile = jnp.concatenate(both * 4, axis=0)
+    for i in range(gram.shape[0] // 8):
+        gram[8 * i : 8 * i + 8, :] = tile
 
 
 def sum_copies(parts):
@@ -531,19 +546,14 @@
     return total + pltpu.roll(total, 2, 0)
 
 
-def middle_kernel(parts, out):
-    total = sum_copies(parts)
-    for i in range(out.shape[0] // 8):
-        out[8 * i : 8 * i + 8, :] = total
-
-
 def total_kernel(parts, out):
     total = sum_copies(parts)
-    rows = jnp.where(row_of((BANDS, LANES)) < 8, total[0:1], total[1:2])
-    own = (row_of((BANDS, LANES)) & 7) == lane_of((BANDS, LANES)) // BANDS
-    fold = (row_of((LANES, BANDS)) & 15) == lane_of((LANES, BANDS))
-    square = dot(jnp.where(own, rows, 0.0), fold.astype(jnp.float32), ((1,), (0,)))
-    out[...] = square * (1.0 / (GX * GY * 1024))
+    total = total * (1.0 / (GX * GY * 1024))
+    row, lane = row_of((BANDS, LANES)), lane_of((BANDS, LANES))
+    rows = jnp.where(row < 8, total[0:1], total[1:2])
+    rows = jnp.where((row & 7) == (lane & 7), rows, 0.0)
+    fold = row_of((LANES, BANDS)) // 8 == lane_of((LANES, BANDS))
+    out[...] = dot(rows, fold.astype(jnp.float32), ((1,), (0,)))
 
 
 def in_hbm(x):
@@ -608,6 +618,27 @@
     )(held, low_in, high_in, sphere, rolled, atom_list)
 
 
+def unpack_call(back):
+    return pl.pallas_call(
+        unpack_kernel,
+        out_shape=(f32(BANDS, 8, 8, LANES), f32(2 * DEVICES, LANES)),
+        in_specs=[VMEM],
+        out_specs=(VMEM, VMEM),
+        compiler_params=params(16),
+        name="unpack",
+    )(back)
+
+
+def total_call(parts):
+    return pl.pallas_call(
+        total_kernel,
+        out_shape=f32(BANDS, BANDS),
+        in_specs=[VMEM],
+        out_specs=VMEM,
+        name="total",
+    )(parts)
+
+
 def shards(wave, potential, positions, species, counts, offsets, beta, coupling):
     packed = pl.pallas_call(
         pack_kernel,
@@ -647,25 +678,11 @@
     atoms = atoms_call(held, offsets.reshape(-1, offsets.shape[2]), beta, coupling[None])
     filtered = filter_call(held, low_in, high_in, *atoms)
     back = lax.all_to_all(filtered, ("slab", "row"), split_axis=0, concat_axis=0, tiled=True)
-    result, partial = pl.pallas_call(
-        unpack_kernel,
-        out_shape=(f32(*wave.shape), f32(512, LANES)),
-        in_specs=[VMEM],
-        out_specs=(VMEM, VMEM),
-        compiler_params=params(16),
-        name="unpack",
-    )(back)
-
+    result, partial = unpack_call(back)
     parts = lax.all_to_all(
         partial, ("slab", "row", "col"), split_axis=0, concat_axis=0, tiled=True
     )
-    gram = pl.pallas_call(
-        total_kernel,
-        out_shape=f32(BANDS, BANDS),
-        in_specs=[VMEM],
-        out_specs=VMEM,
-        name="total",
-    )(parts)
+    gram = total_call(parts)
     return result, gram
 
 

time: 136 us -> 136 us (level)
  Pallas kernels: 32.6 us -> 29.9 us
  blocking collectives: 83.1 us -> 85 us
    all_to_all x1, blocking collectives: 16.9 us -> 18.7 us  [shards(): lax.all_to_all(filtered, ('slab', 'row'), split_axis=0, concat_axis=0, ti...]
where the time goes in v4:
time: 136 us; the launch traced here: 135 us
  blocking collectives  85 us (62%)
  Pallas kernels  29.9 us (22%)
  starting transfers between devices  16.7 us (12%)
  waiting for transfers between devices  2.38 us (2%)
  between operations  1.37 us (1%)
    all_to_all x1, blocking collectives, shards(): lax.all_to_all(packed, ('slab', 'row'), split_axis=0, concat_axis=0, tile...  38.8 us
    all_to_all x1, blocking collectives, shards(): lax.all_to_all(partial, ('slab', 'row', 'col'), split_axis=0, concat_axis...  27.5 us
    all_to_all x1, blocking collectives, shards(): lax.all_to_all(filtered, ('slab', 'row'), split_axis=0, concat_axis=0, ti...  18.7 us
    pallas_call x1, Pallas kernels, filter_call(): pl.pallas_call(filter_kernel, out_shape=f32(BLOCKS, 4, 8, LANES), in_spec...  18.6 us
    ppermute x1, starting transfers between devices, shards(): low_in = lax.ppermute(high_edge, ('slab', 'col'), up)  14.8 us
    pallas_call x1, Pallas kernels, atoms_call(): pl.pallas_call(atoms_kernel, out_shape=(pltpu.VMEM((beta.shape[0], TILES...  6.29 us
  transfers between devices with their start and end apart: 2, of which 1 were waited for; matrix products, arithmetic and copies ran while one was open for 0% of the time, Pallas kernels for 5%

profile of v4, /device:TPU:1, one launch (start us, length us, event | category | flops | bytes accessed | tf_op | source)
XLA Modules:
  0.0 135.3 jit_solution(16892403653436442045)
XLA Ops:
  1.3 1.4 %pack.1 = f32[32,9,8,128]{3,2,1,0:T(8,128)S(1)} custom-call(s32[3,8]{1,0:T(4,128)} %positions_in.1, s32[1,8]{1,0:T(1,128)} %bitcast.9, s32[1,1]{1,0:T(1,128)} %bitcast.5.counts_in, f32[16,8,8,128]{3,2,1,0:T(8,128)} %wave_in.1, f32[8,8,128]{2,1,0:T(8,128)} %potential_in.1), custom_call_target="tpu_custom_call" | custom-call | tf_op jit(solution)/shard_map/pack/pallas_call | solution.py:643
  2.7 38.8 %all_to_all.21.held = f32[32,9,8,128]{3,2,1,0:T(8,128)S(1)} all-to-all(f32[32,9,8,128]{3,2,1,0:T(8,128)S(1)} %pack.1), channel_id=1, replica_groups=mesh['slab'=4,'row'=8,'col'=8] {'slab','row'}, dimensions={0} | all-to-all | bytes 2359296 | tf_op jit(solution)/shard_map/all_to_all | solution.py:660
  41.5 0.0 copy-start.2
  41.5 0.0 copy-start
  41.5 0.0 copy-start.1
  41.5 0.7 edges.1
  42.2 14.8 %collective-permute-start = (f32[1056,128]{1,0:T(8,128)S(1)}, f32[1056,128]{1,0:T(8,128)S(1)}, u32[]{:S(2)}, u32[]{:S(2)}) collective-permute-start(f32[1056,128]{1,0:T(8,128)S(1)} %get-tuple-element.9), channel_id=1, source_target_pairs={{0,64},{64,65},{65,129},{129,130},{130,194},{194,195},{195,3},{3,4... | collective-permute-start | bytes 1622024 | tf_op jit(solution)/shard_map/ppermute | solution.py:675
  57.0 1.9 %collective-permute-start.1 = (f32[1056,128]{1,0:T(8,128)S(1)}, f32[1056,128]{1,0:T(8,128)S(1)}, u32[]{:S(2)}, u32[]{:S(2)}) collective-permute-start(f32[1056,128]{1,0:T(8,128)S(1)} %get-tuple-element.10), channel_id=1, source_target_pairs={{64,0},{65,64},{129,65},{130,129},{194,130},{195,194},{3,195},{4,3... | collective-permute-start | bytes 1622024 | tf_op jit(solution)/shard_map/ppermute | solution.py:676
  58.9 0.0 copy-done.2
  59.0 0.0 copy-done
  59.0 0.0 copy-done.1
  59.0 6.3 %atoms.1 = (f32[4,88,128]{2,1,0:T(8,128)S(1)}, f32[264,88,128]{2,1,0:T(8,128)S(1)}, s32[1024]{0:T(1024)S(1)}) custom-call(f32[32,9,8,128]{3,2,1,0:T(8,128)S(1)} %all_to_all.21.held, s32[12,384]{1,0:T(8,128)S(1)} %reshape.9.offsets, f32[4,384]{1,0:T(4,128)S(1)} %copy-done, f32[1,4]{1,0:T(1,128)S(1)} %bitcast.7), custom_call_target="tpu_custom_call" | custom-call | flops 100000000 | bytes 10000000 | tf_op jit(solution)/shard_map/atoms/pallas_call | solution.py:575
  65.3 0.0 collective-permute-done.low_in
  65.3 2.4 %collective-permute-done.1.high_in = f32[1056,128]{1,0:T(8,128)S(1)} collective-permute-done((f32[1056,128]{1,0:T(8,128)S(1)}, f32[1056,128]{1,0:T(8,128)S(1)}, u32[]{:S(2)}, u32[]{:S(2)}) %collective-permute-start.1) | collective-permute-done | bytes 540704 | tf_op jit(solution)/shard_map/ppermute | solution.py:676
  67.7 18.6 %filter.1 = f32[32,4,8,128]{3,2,1,0:T(8,128)S(1)} custom-call(f32[32,9,8,128]{3,2,1,0:T(8,128)S(1)} %all_to_all.21.held, f32[1056,128]{1,0:T(8,128)S(1)} %collective-permute-done.low_in, f32[1056,128]{1,0:T(8,128)S(1)} %collective-permute-done.1.high_in, f32[4,88,128]{2,1,0:T(8,128)S(1)} %get-tuple-element.11.sphere, ...), custom_call_target="tpu_custom_call" | custom-call | tf_op jit(solution)/shard_map/filter/pallas_call | solution.py:597
  86.3 18.7 %all_to_all.22.held = f32[32,4,8,128]{3,2,1,0:T(8,128)S(1)} all-to-all(f32[32,4,8,128]{3,2,1,0:T(8,128)S(1)} %filter.1), channel_id=1, replica_groups=mesh['slab'=4,'row'=8,'col'=8] {'slab','row'}, dimensions={0} | all-to-all | bytes 1048576 | tf_op jit(solution)/shard_map/all_to_all | solution.py:680
  104.9 1.2 unpack.1
  106.1 27.5 %all_to_all.23 = f32[256,2,128]{2,1,0:T(2,128)} all-to-all(f32[256,2,128]{2,1,0:T(2,128)S(1)} %bitcast.6), channel_id=1, replica_groups=mesh['slab'=4,'row'=8,'col'=8] {'slab','row','col'}, dimensions={0} | all-to-all | bytes 524288 | tf_op jit(solution)/shard_map/all_to_all | solution.py:682
  133.6 1.7 %total.1 = f32[16,16]{1,0:T(8,128)} custom-call(f32[512,128]{1,0:T(8,128)} %bitcast.8), custom_call_target="tpu_custom_call" | custom-call | tf_op jit(solution)/shard_map/total/pallas_call | solution.py:633
  (2 shorter events, 0.0 us)
Async XLA Ops:
  41.5 17.4 %copy-start.2 = (s32[4,3,384]{2,0,1:T(4,128)S(1)}, s32[4,3,384]{2,0,1:T(4,128)}, u32[]{:S(2)}) copy-start(s32[4,3,384]{2,0,1:T(4,128)} %param.13) | copy-start | bytes 55300
  41.5 17.5 %copy-start = (f32[4,384]{1,0:T(4,128)S(1)}, f32[4,384]{1,0:T(4,128)}, u32[]{:S(2)}) copy-start(f32[4,384]{1,0:T(4,128)} %beta.1) | copy-start | bytes 18436
  41.5 17.5 %copy-start.1 = (f32[4]{0:T(128)S(1)}, f32[4]{0:T(128)}, u32[]{:S(2)}) copy-start(f32[4]{0:T(128)} %param.15) | copy-start | bytes 52
  42.2 23.1 %collective-permute-start = (f32[1056,128]{1,0:T(8,128)S(1)}, f32[1056,128]{1,0:T(8,128)S(1)}, u32[]{:S(2)}, u32[]{:S(2)}) collective-permute-start(f32[1056,128]{1,0:T(8,128)S(1)} %get-tuple-element.9), channel_id=1, source_target_pairs={{0,64},{64,65},{65,129},{129,130},{130,194},{194,195},{195,3},{3,4... | collective-permute-start | bytes 1622024 | tf_op jit(solution)/shard_map/ppermute | solution.py:675
  57.0 10.7 %collective-permute-start.1 = (f32[1056,128]{1,0:T(8,128)S(1)}, f32[1056,128]{1,0:T(8,128)S(1)}, u32[]{:S(2)}, u32[]{:S(2)}) collective-permute-start(f32[1056,128]{1,0:T(8,128)S(1)} %get-tuple-element.10), channel_id=1, source_target_pairs={{64,0},{65,64},{129,65},{130,129},{194,130},{195,194},{3,195},{4,3... | collective-permute-start | bytes 1622024 | tf_op jit(solution)/shard_map/ppermute | solution.py:676
